TPU v7x, 512 devices: a whole 4x4x16 slice. The times are simulated.
512 devices in a mesh: gx: 16 (over z), gy: 32 (over y, x, core).
Axes of the slice: x: 4, y: 4, z: 16, core: 2. Of those that a mesh axis runs over, the one named last changes fastest.
Arguments:
- source: float32 [128, 256, 256], P('gx', 'gy'), may hold values from -5 to 5
- kappa: float32 [128, 256, 256], P('gx', 'gy'), may hold values from 0.3 to 3
Outputs:
- fine_solution: float32 [128, 256, 256], P('gx', 'gy')
- coarse_solution: float32 [64, 128, 128], P('gx', 'gy')
All inputs are finite; a program needn't handle non-finite values.
Results may differ from a plain program's by a relative error of at most 0.00015.
Values sent between devices are 32-bit elements; how exact they have to be, the bound alone decides.
A program may use at most 64 MiB of HBM per device.

v0:
```python
import jax
import jax.numpy as jnp
from jax import lax
from jax.sharding import PartitionSpec as P

LEVELS = 3
PRE = 2
POST = 2
CSWEEPS = 8


OMEGA = 0.8


def with_halo(cells, sides, width):
    for axis, dim in sides:
        count = lax.axis_size(axis)
        ends = count - 1
        head = lax.slice_in_dim(cells, 0, width, axis=dim)
        tail = lax.slice_in_dim(cells, cells.shape[dim] - width, cells.shape[dim], axis=dim)
        cells = jnp.concatenate(
            [
                lax.ppermute(tail, axis, [(i, (i + 1) % count) for i in range(ends)]),
                cells,
                lax.ppermute(head, axis, [((i + 1) % count, i) for i in range(ends)]),
            ],
            axis=dim,
        )
    return cells


def restrict(field):
    lead = field.shape[:-3]
    size_a, size_b, size_c = field.shape[-3:]
    blocks = field.reshape(lead + (size_a // 2, 2, size_b // 2, 2, size_c // 2, 2))
    return blocks.mean(axis=(-5, -3, -1))


def prolong(field):
    return jnp.repeat(jnp.repeat(jnp.repeat(field, 2, -3), 2, -2), 2, -1)


def stencil_faces(padded):
    centre = padded[..., 1:-1, 1:-1, 1:-1]
    face_west = 0.5 * (centre + padded[..., :-2, 1:-1, 1:-1])
    face_east = 0.5 * (centre + padded[..., 2:, 1:-1, 1:-1])
    face_south = 0.5 * (centre + padded[..., 1:-1, :-2, 1:-1])
    face_north = 0.5 * (centre + padded[..., 1:-1, 2:, 1:-1])
    face_below = 0.5 * (centre + padded[..., 1:-1, 1:-1, :-2])
    face_above = 0.5 * (centre + padded[..., 1:-1, 1:-1, 2:])
    total = face_west + face_east + face_south + face_north + face_below + face_above
    return (face_west, face_east, face_south, face_north, face_below, face_above, total)


def neighbours(padded, field, coeff):
    beside = coeff[0] * padded[..., :-2, 1:-1, 1:-1] + coeff[1] * padded[..., 2:, 1:-1, 1:-1]
    beside = (
        beside + coeff[2] * padded[..., 1:-1, :-2, 1:-1] + coeff[3] * padded[..., 1:-1, 2:, 1:-1]
    )
    beside = (
        beside + coeff[4] * padded[..., 1:-1, 1:-1, :-2] + coeff[5] * padded[..., 1:-1, 1:-1, 2:]
    )
    return coeff[6] * field - beside


def operate_local(field, coeff):
    rimmed = with_halo(field, (("gx", 1), ("gy", 2)), 1)
    padded = jnp.pad(rimmed, ((0, 0), (0, 0), (0, 0), (1, 1)))
    return neighbours(padded, field, coeff)


def operate_whole(field, coeff):
    padded = jnp.pad(field, ((0, 0), (1, 1), (1, 1), (1, 1)))
    return neighbours(padded, field, coeff)


def sweeps(field, rhs_field, coeff, count, operator):
    for repeat in range(count):
        field = field + OMEGA * (rhs_field - operator(field, coeff)) / coeff[6]
    return field


def inner(left, right):
    return jnp.sum(left * right, axis=(-3, -2, -1), keepdims=True)


def conjgrad(rhs_field, coeff):
    field = jnp.zeros_like(rhs_field)
    resid = rhs_field
    direction = rhs_field
    norm_now = inner(resid, resid)
    for repeat in range(CSWEEPS):
        image = operate_whole(direction, coeff)
        alpha = norm_now / inner(direction, image)
        field = field + alpha * direction
        resid = resid - alpha * image
        norm_next = inner(resid, resid)
        direction = resid + norm_next / norm_now * direction
        norm_now = norm_next
    return field


def agglomerate(field):
    width_x = lax.axis_size("gx")
    width_y = lax.axis_size("gy")
    stack_size, cells_x, cells_y, cells_z = field.shape
    pooled = lax.all_gather(field[None], ("gx", "gy"), axis=0, tiled=True)
    pooled = pooled.reshape(width_x, width_y, stack_size, cells_x, cells_y, cells_z)
    pooled = pooled.transpose(2, 0, 3, 1, 4, 5)
    return pooled.reshape(stack_size, width_x * cells_x, width_y * cells_y, cells_z)


def descend(section, rhs_field, coeffs):
    coeff = coeffs[section]
    if section == LEVELS:
        whole_rhs = agglomerate(rhs_field)
        field = conjgrad(whole_rhs, coeff)
        zero_index = jnp.zeros((), jnp.int32)
        start_x = lax.axis_index("gx") * rhs_field.shape[1]
        start_y = lax.axis_index("gy") * rhs_field.shape[2]
        return lax.dynamic_slice(field, (zero_index, start_x, start_y, zero_index), rhs_field.shape)
    field = OMEGA * rhs_field / coeff[6]
    field = sweeps(field, rhs_field, coeff, PRE - 1, operate_local)
    resid = rhs_field - operate_local(field, coeff)
    correction = descend(section + 1, 4.0 * restrict(resid), coeffs)
    field = field + prolong(correction)
    return sweeps(field, rhs_field, coeff, POST, operate_local)


def on_device(source, kappa):
    kappas = [kappa]
    for section in range(LEVELS):
        kappas.append(restrict(kappas[-1]))
    coeffs = []
    for section in range(LEVELS):
        rimmed = with_halo(kappas[section], (("gx", 0), ("gy", 1)), 1)
        coeffs.append(stencil_faces(jnp.pad(rimmed, ((0, 0), (0, 0), (1, 1)))))
    whole_kappa = agglomerate(kappas[LEVELS][None])[0]
    coeffs.append(stencil_faces(jnp.pad(whole_kappa, 1)))
    fine_rhs = source[None]
    field = descend(0, fine_rhs, coeffs)
    coarse_field = descend(1, 4.0 * restrict(fine_rhs), coeffs)
    return (field[0], coarse_field[0])


def solution(mesh):
    in_specs = (P("gx", "gy", None), P("gx", "gy", None))
    out_specs = (P("gx", "gy", None), P("gx", "gy", None))
    return jax.shard_map(
        on_device, mesh=mesh, in_specs=in_specs, out_specs=out_specs, check_vma=False
    )
```

profile of v0, /device:TPU:103, one launch (start us, length us, event | category | flops | bytes accessed | tf_op | source)
XLA Modules:
  0.0 967.2 jit_solution(3182763332869224246)
XLA Ops:
  7.2 6.3 reshape.421
  16.1 4.8 collective-permute-start.12
  23.4 4.6 collective-permute-start.24
  29.9 4.6 collective-permute-start
  34.5 5.5 reshape_broadcast_in_dim.3
  44.6 5.1 collective-permute-start.14
  51.7 5.8 collective-permute-start.26
  59.6 4.9 collective-permute-start.60
  66.5 3.5 collective-permute-done.61
  70.1 7.2 collective-permute-start.62
  79.2 5.0 collective-permute-done.63
  97.0 5.8 collective-permute-start.2
  105.7 4.2 collective-permute-done.3
  110.2 4.0 collective-permute-start.4
  116.2 4.9 collective-permute-start.68
  127.9 5.0 collective-permute-done.7
  133.2 4.9 collective-permute-start.8
  140.1 3.6 collective-permute-done.9
  149.1 5.8 collective-permute-start.70
  157.1 5.5 reshape.420
  172.8 6.9 collective-permute-start.18
  181.7 5.0 collective-permute-done.19
  202.6 5.1 collective-permute-done.23
  208.5 4.4 collective-permute-start.28
  219.3 5.6 collective-permute-start.30
  226.9 5.0 collective-permute-done.31
  232.1 4.9 collective-permute-start.32
  248.1 4.8 collective-permute-done.35
  254.1 449.2 %all-reduce.46.cloned.1.call-done = (f32[16384]{0:T(1024)}, f32[16384]{0:T(1024)}, f32[16384]{0:T(1024)}) async-done(((f32[16384]{0:T(1024)}, f32[16384]{0:T(1024)}, f32[16384]{0:T(1024)}), (f32[16384]{0:T(1024)}, f32[16384]{0:T(1024)}, f32[16384]{0:T(1024)})) %all-reduce.46.cloned.1.call-update) | async-done | bytes 196624
  803.7 4.4 collective-permute-start.78
  810.0 5.8 collective-permute-start.38
  818.6 4.9 collective-permute-start.80
  826.3 4.6 collective-permute-start.40
  832.9 6.6 collective-permute-start.82
  841.4 5.8 collective-permute-start.42
  856.2 4.8 collective-permute-start.44
  862.9 4.6 collective-permute-start.84
  869.5 3.5 collective-permute-start.46
  874.9 5.8 collective-permute-start.86
  883.6 4.9 collective-permute-start.48
  890.6 3.5 collective-permute-done.49
  894.0 7.2 collective-permute-start.50
  904.0 4.2 collective-permute-done.51
  925.7 5.8 collective-permute-start.90
  934.6 4.1 collective-permute-start.56
  940.7 3.5 collective-permute-done.57
  944.3 7.2 collective-permute-start.58
  954.9 3.7 collective-permute-done.59
  (420 shorter events, 225.3 us)
Async XLA Ops:
  7.2 696.1 %all-reduce.46.cloned.1.call-start = ((), (), s32[]{:S(2)}) async-start(), calls=%async_computation | async-start | bytes 393216
  16.1 28.5 %collective-permute-start.12 = (f32[1,4,128]{2,1,0:T(4,128)S(1)}, f32[1,4,128]{2,1,0:T(4,128)S(1)}, u32[]{:S(2)}, u32[]{:S(2)}) collective-permute-start(f32[1,4,128]{2,1,0:T(4,128)S(1)} %get-tuple-element.154), channel_id=1, source_target_pairs={{0,32},{32,64},{64,96},{96,128},{128,160},{160,192},{192,224},{224... | collective-permute-start | bytes 6152 | tf_op jit(solution)/shard_map/ppermute | solution.py:23
  20.8 23.8 %collective-permute-start.13 = (f32[1,4,128]{2,1,0:T(4,128)S(1)}, f32[1,4,128]{2,1,0:T(4,128)S(1)}, u32[]{:S(2)}, u32[]{:S(2)}) collective-permute-start(f32[1,4,128]{2,1,0:T(4,128)S(1)} %get-tuple-element.155), channel_id=1, source_target_pairs={{32,0},{64,32},{96,64},{128,96},{160,128},{192,160},{224,192},{256... | collective-permute-start | bytes 6152 | tf_op jit(solution)/shard_map/ppermute | solution.py:25
  23.4 19.2 %collective-permute-start.24 = (f32[1,2,64]{2,1,0:T(2,128)S(1)}, f32[1,2,64]{2,1,0:T(2,128)S(1)}, u32[]{:S(2)}, u32[]{:S(2)}) collective-permute-start(f32[1,2,64]{2,1,0:T(2,128)S(1)} %get-tuple-element.191), channel_id=1, source_target_pairs={{0,32},{32,64},{64,96},{96,128},{128,160},{160,192},{192,224},{224... | collective-permute-start | bytes 1544 | tf_op jit(solution)/shard_map/ppermute | solution.py:23
  28.0 16.6 %collective-permute-start.25 = (f32[1,2,64]{2,1,0:T(2,128)S(1)}, f32[1,2,64]{2,1,0:T(2,128)S(1)}, u32[]{:S(2)}, u32[]{:S(2)}) collective-permute-start(f32[1,2,64]{2,1,0:T(2,128)S(1)} %get-tuple-element.192), channel_id=1, source_target_pairs={{32,0},{64,32},{96,64},{128,96},{160,128},{192,160},{224,192},{256... | collective-permute-start | bytes 1544 | tf_op jit(solution)/shard_map/ppermute | solution.py:25
  29.9 49.2 %collective-permute-start = (f32[1,8,256]{2,1,0:T(8,128)S(1)}, f32[1,8,256]{2,1,0:T(8,128)S(1)}, u32[]{:S(2)}, u32[]{:S(2)}) collective-permute-start(f32[1,8,256]{2,1,0:T(8,128)S(1)} %get-tuple-element.119), channel_id=1, source_target_pairs={{0,32},{32,64},{64,96},{96,128},{128,160},{160,192},{192,224},{224... | collective-permute-start | bytes 24584 | tf_op jit(solution)/shard_map/ppermute | solution.py:23
  42.6 47.1 %collective-permute-start.1 = (f32[1,8,256]{2,1,0:T(8,128)S(1)}, f32[1,8,256]{2,1,0:T(8,128)S(1)}, u32[]{:S(2)}, u32[]{:S(2)}) collective-permute-start(f32[1,8,256]{2,1,0:T(8,128)S(1)} %get-tuple-element.118), channel_id=1, source_target_pairs={{32,0},{64,32},{96,64},{128,96},{160,128},{192,160},{224,192},{256... | collective-permute-start | bytes 24584 | tf_op jit(solution)/shard_map/ppermute | solution.py:25
  44.6 12.8 %collective-permute-start.14 = (f32[6,1,128]{2,1,0:T(1,128)S(1)}, f32[6,1,128]{2,1,0:T(1,128)S(1)}, u32[]{:S(2)}, u32[]{:S(2)}) collective-permute-start(f32[6,1,128]{2,1,0:T(1,128)S(1)} %get-tuple-element.137), channel_id=1, source_target_pairs={{0,1},{1,2},{2,3},{3,4},{4,5},{5,6},{6,7},{7,8},{8,9},{9,10},{10,1... | collective-permute-start | bytes 9224 | tf_op jit(solution)/shard_map/ppermute | solution.py:23
  49.7 9.6 collective-permute-start.15
  51.7 12.8 %collective-permute-start.26 = (f32[4,1,64]{2,1,0:T(1,128)S(1)}, f32[4,1,64]{2,1,0:T(1,128)S(1)}, u32[]{:S(2)}, u32[]{:S(2)}) collective-permute-start(f32[4,1,64]{2,1,0:T(1,128)S(1)} %get-tuple-element.173), channel_id=1, source_target_pairs={{0,1},{1,2},{2,3},{3,4},{4,5},{5,6},{6,7},{7,8},{8,9},{9,10},{10,1... | collective-permute-start | bytes 3080 | tf_op jit(solution)/shard_map/ppermute | solution.py:23
  92.0 12.8 %collective-permute-start.66 = (f32[1,6,1,128]{3,2,1,0:T(1,128)S(1)}, f32[1,6,1,128]{3,2,1,0:T(1,128)S(1)}, u32[]{:S(2)}, u32[]{:S(2)}) collective-permute-start(f32[1,6,1,128]{3,2,1,0:T(1,128)S(1)} %get-tuple-element.128), channel_id=1, source_target_pairs={{0,1},{1,2},{2,3},{3,4},{4,5},{5,6},{6,7},{7,8},{8,9},{9,10},{10,1... | collective-permute-start | bytes 9224 | tf_op jit(solution)/shard_map/ppermute | solution.py:23
  95.1 9.7 collective-permute-start.67
  110.2 13.0 %collective-permute-start.4 = (f32[1,1,8,256]{3,2,1,0:T(8,128)S(1)}, f32[1,1,8,256]{3,2,1,0:T(8,128)S(1)}, u32[]{:S(2)}, u32[]{:S(2)}) collective-permute-start(f32[1,1,8,256]{3,2,1,0:T(8,128)S(1)} %get-tuple-element.116), channel_id=1, source_target_pairs={{0,32},{32,64},{64,96},{96,128},{128,160},{160,192},{192,224},{224... | collective-permute-start | bytes 24584 | tf_op jit(solution)/shard_map/ppermute | solution.py:23
  116.2 23.8 %collective-permute-start.68 = (f32[1,1,2,64]{3,2,1,0:T(2,128)S(1)}, f32[1,1,2,64]{3,2,1,0:T(2,128)S(1)}, u32[]{:S(2)}, u32[]{:S(2)}) collective-permute-start(f32[1,1,2,64]{3,2,1,0:T(2,128)S(1)} %get-tuple-element.184), channel_id=1, source_target_pairs={{0,32},{32,64},{64,96},{96,128},{128,160},{160,192},{192,224},{224... | collective-permute-start | bytes 1544 | tf_op jit(solution)/shard_map/ppermute | solution.py:23
  121.1 18.9 %collective-permute-start.69 = (f32[1,1,2,64]{3,2,1,0:T(2,128)S(1)}, f32[1,1,2,64]{3,2,1,0:T(2,128)S(1)}, u32[]{:S(2)}, u32[]{:S(2)}) collective-permute-start(f32[1,1,2,64]{3,2,1,0:T(2,128)S(1)} %get-tuple-element.185), channel_id=1, source_target_pairs={{32,0},{64,32},{96,64},{128,96},{160,128},{192,160},{224,192},{256... | collective-permute-start | bytes 1544 | tf_op jit(solution)/shard_map/ppermute | solution.py:25
  143.7 13.0 %collective-permute-start.10 = (f32[1,10,1,256]{3,2,1,0:T(1,128)S(1)}, f32[1,10,1,256]{3,2,1,0:T(1,128)S(1)}, u32[]{:S(2)}, u32[]{:S(2)}) collective-permute-start(f32[1,10,1,256]{3,2,1,0:T(1,128)S(1)} %get-tuple-element.104), channel_id=1, source_target_pairs={{0,1},{1,2},{2,3},{3,4},{4,5},{5,6},{6,7},{7,8},{8,9},{9,10},{10,1... | collective-permute-start | bytes 30728 | tf_op jit(solution)/shard_map/ppermute | solution.py:23
  149.1 21.5 %collective-permute-start.70 = (f32[1,4,1,64]{3,2,1,0:T(1,128)S(1)}, f32[1,4,1,64]{3,2,1,0:T(1,128)S(1)}, u32[]{:S(2)}, u32[]{:S(2)}) collective-permute-start(f32[1,4,1,64]{3,2,1,0:T(1,128)S(1)} %get-tuple-element.166), channel_id=1, source_target_pairs={{0,1},{1,2},{2,3},{3,4},{4,5},{5,6},{6,7},{7,8},{8,9},{9,10},{10,1... | collective-permute-start | bytes 3080 | tf_op jit(solution)/shard_map/ppermute | solution.py:23
  154.8 15.8 %collective-permute-start.71 = (f32[1,4,1,64]{3,2,1,0:T(1,128)S(1)}, f32[1,4,1,64]{3,2,1,0:T(1,128)S(1)}, u32[]{:S(2)}, u32[]{:S(2)}) collective-permute-start(f32[1,4,1,64]{3,2,1,0:T(1,128)S(1)} %get-tuple-element.167), channel_id=1, source_target_pairs={{1,0},{2,1},{3,2},{4,3},{5,4},{6,5},{7,6},{8,7},{9,8},{10,9},{11,1... | collective-permute-start | bytes 3080 | tf_op jit(solution)/shard_map/ppermute | solution.py:25
  186.9 10.6 %collective-permute-start.20 = (f32[1,1,4,128]{3,2,1,0:T(4,128)S(1)}, f32[1,1,4,128]{3,2,1,0:T(4,128)S(1)}, u32[]{:S(2)}, u32[]{:S(2)}) collective-permute-start(f32[1,1,4,128]{3,2,1,0:T(4,128)S(1)} %get-tuple-element.150), channel_id=1, source_target_pairs={{0,32},{32,64},{64,96},{96,128},{128,160},{160,192},{192,224},{224... | collective-permute-start | bytes 6152 | tf_op jit(solution)/shard_map/ppermute | solution.py:23
  192.2 10.3 %collective-permute-start.72 = (f32[1,1,2,64]{3,2,1,0:T(2,128)S(1)}, f32[1,1,2,64]{3,2,1,0:T(2,128)S(1)}, u32[]{:S(2)}, u32[]{:S(2)}) collective-permute-start(f32[1,1,2,64]{3,2,1,0:T(2,128)S(1)} %get-tuple-element.182), channel_id=1, source_target_pairs={{0,32},{32,64},{64,96},{96,128},{128,160},{160,192},{192,224},{224... | collective-permute-start | bytes 1544 | tf_op jit(solution)/shard_map/ppermute | solution.py:23
  208.5 10.7 %collective-permute-start.28 = (f32[1,1,2,64]{3,2,1,0:T(2,128)S(1)}, f32[1,1,2,64]{3,2,1,0:T(2,128)S(1)}, u32[]{:S(2)}, u32[]{:S(2)}) collective-permute-start(f32[1,1,2,64]{3,2,1,0:T(2,128)S(1)} %get-tuple-element.189), channel_id=1, source_target_pairs={{0,32},{32,64},{64,96},{96,128},{128,160},{160,192},{192,224},{224... | collective-permute-start | bytes 1544 | tf_op jit(solution)/shard_map/ppermute | solution.py:23
  214.9 11.9 %collective-permute-start.74 = (f32[1,4,1,64]{3,2,1,0:T(1,128)S(1)}, f32[1,4,1,64]{3,2,1,0:T(1,128)S(1)}, u32[]{:S(2)}, u32[]{:S(2)}) collective-permute-start(f32[1,4,1,64]{3,2,1,0:T(1,128)S(1)} %get-tuple-element.164), channel_id=1, source_target_pairs={{0,1},{1,2},{2,3},{3,4},{4,5},{5,6},{6,7},{7,8},{8,9},{9,10},{10,1... | collective-permute-start | bytes 3080 | tf_op jit(solution)/shard_map/ppermute | solution.py:23
  217.2 9.7 %collective-permute-start.75 = (f32[1,4,1,64]{3,2,1,0:T(1,128)S(1)}, f32[1,4,1,64]{3,2,1,0:T(1,128)S(1)}, u32[]{:S(2)}, u32[]{:S(2)}) collective-permute-start(f32[1,4,1,64]{3,2,1,0:T(1,128)S(1)} %get-tuple-element.165), channel_id=1, source_target_pairs={{1,0},{2,1},{3,2},{4,3},{5,4},{6,5},{7,6},{8,7},{9,8},{10,9},{11,1... | collective-permute-start | bytes 3080 | tf_op jit(solution)/shard_map/ppermute | solution.py:25
  790.1 13.5 %collective-permute-start.76 = (f32[1,1,2,64]{3,2,1,0:T(2,128)S(1)}, f32[1,1,2,64]{3,2,1,0:T(2,128)S(1)}, u32[]{:S(2)}, u32[]{:S(2)}) collective-permute-start(f32[1,1,2,64]{3,2,1,0:T(2,128)S(1)} %get-tuple-element.176), channel_id=1, source_target_pairs={{0,32},{32,64},{64,96},{96,128},{128,160},{160,192},{192,224},{224... | collective-permute-start | bytes 1544 | tf_op jit(solution)/shard_map/ppermute | solution.py:23
  792.0 11.6 %collective-permute-start.77 = (f32[1,1,2,64]{3,2,1,0:T(2,128)S(1)}, f32[1,1,2,64]{3,2,1,0:T(2,128)S(1)}, u32[]{:S(2)}, u32[]{:S(2)}) collective-permute-start(f32[1,1,2,64]{3,2,1,0:T(2,128)S(1)} %get-tuple-element.177), channel_id=1, source_target_pairs={{32,0},{64,32},{96,64},{128,96},{160,128},{192,160},{224,192},{256... | collective-permute-start | bytes 1544 | tf_op jit(solution)/shard_map/ppermute | solution.py:25
  798.3 11.6 %collective-permute-start.36 = (f32[1,1,2,64]{3,2,1,0:T(2,128)S(1)}, f32[1,1,2,64]{3,2,1,0:T(2,128)S(1)}, u32[]{:S(2)}, u32[]{:S(2)}) collective-permute-start(f32[1,1,2,64]{3,2,1,0:T(2,128)S(1)} %get-tuple-element.180), channel_id=1, source_target_pairs={{0,32},{32,64},{64,96},{96,128},{128,160},{160,192},{192,224},{224... | collective-permute-start | bytes 1544 | tf_op jit(solution)/shard_map/ppermute | solution.py:23
  803.7 14.0 %collective-permute-start.78 = (f32[1,4,1,64]{3,2,1,0:T(1,128)S(1)}, f32[1,4,1,64]{3,2,1,0:T(1,128)S(1)}, u32[]{:S(2)}, u32[]{:S(2)}) collective-permute-start(f32[1,4,1,64]{3,2,1,0:T(1,128)S(1)} %get-tuple-element.158), channel_id=1, source_target_pairs={{0,1},{1,2},{2,3},{3,4},{4,5},{5,6},{6,7},{7,8},{8,9},{9,10},{10,1... | collective-permute-start | bytes 3080 | tf_op jit(solution)/shard_map/ppermute | solution.py:23
  808.0 9.7 %collective-permute-start.79 = (f32[1,4,1,64]{3,2,1,0:T(1,128)S(1)}, f32[1,4,1,64]{3,2,1,0:T(1,128)S(1)}, u32[]{:S(2)}, u32[]{:S(2)}) collective-permute-start(f32[1,4,1,64]{3,2,1,0:T(1,128)S(1)} %get-tuple-element.159), channel_id=1, source_target_pairs={{1,0},{2,1},{3,2},{4,3},{5,4},{6,5},{7,6},{8,7},{9,8},{10,9},{11,1... | collective-permute-start | bytes 3080 | tf_op jit(solution)/shard_map/ppermute | solution.py:25
  810.0 15.4 %collective-permute-start.38 = (f32[1,4,1,64]{3,2,1,0:T(1,128)S(1)}, f32[1,4,1,64]{3,2,1,0:T(1,128)S(1)}, u32[]{:S(2)}, u32[]{:S(2)}) collective-permute-start(f32[1,4,1,64]{3,2,1,0:T(1,128)S(1)} %get-tuple-element.162), channel_id=1, source_target_pairs={{0,1},{1,2},{2,3},{3,4},{4,5},{5,6},{6,7},{7,8},{8,9},{9,10},{10,1... | collective-permute-start | bytes 3080 | tf_op jit(solution)/shard_map/ppermute | solution.py:23
  818.6 14.2 %collective-permute-start.80 = (f32[1,1,2,64]{3,2,1,0:T(2,128)S(1)}, f32[1,1,2,64]{3,2,1,0:T(2,128)S(1)}, u32[]{:S(2)}, u32[]{:S(2)}) collective-permute-start(f32[1,1,2,64]{3,2,1,0:T(2,128)S(1)} %get-tuple-element.174), channel_id=1, source_target_pairs={{0,32},{32,64},{64,96},{96,128},{128,160},{160,192},{192,224},{224... | collective-permute-start | bytes 1544 | tf_op jit(solution)/shard_map/ppermute | solution.py:23
  826.3 15.1 %collective-permute-start.40 = (f32[1,1,2,64]{3,2,1,0:T(2,128)S(1)}, f32[1,1,2,64]{3,2,1,0:T(2,128)S(1)}, u32[]{:S(2)}, u32[]{:S(2)}) collective-permute-start(f32[1,1,2,64]{3,2,1,0:T(2,128)S(1)} %get-tuple-element.178), channel_id=1, source_target_pairs={{0,32},{32,64},{64,96},{96,128},{128,160},{160,192},{192,224},{224... | collective-permute-start | bytes 1544 | tf_op jit(solution)/shard_map/ppermute | solution.py:23
  830.9 10.5 %collective-permute-start.41 = (f32[1,1,2,64]{3,2,1,0:T(2,128)S(1)}, f32[1,1,2,64]{3,2,1,0:T(2,128)S(1)}, u32[]{:S(2)}, u32[]{:S(2)}) collective-permute-start(f32[1,1,2,64]{3,2,1,0:T(2,128)S(1)} %get-tuple-element.179), channel_id=1, source_target_pairs={{32,0},{64,32},{96,64},{128,96},{160,128},{192,160},{224,192},{256... | collective-permute-start | bytes 1544 | tf_op jit(solution)/shard_map/ppermute | solution.py:25
  832.9 16.3 %collective-permute-start.82 = (f32[1,4,1,64]{3,2,1,0:T(1,128)S(1)}, f32[1,4,1,64]{3,2,1,0:T(1,128)S(1)}, u32[]{:S(2)}, u32[]{:S(2)}) collective-permute-start(f32[1,4,1,64]{3,2,1,0:T(1,128)S(1)} %get-tuple-element.156), channel_id=1, source_target_pairs={{0,1},{1,2},{2,3},{3,4},{4,5},{5,6},{6,7},{7,8},{8,9},{9,10},{10,1... | collective-permute-start | bytes 3080 | tf_op jit(solution)/shard_map/ppermute | solution.py:23
  839.5 9.7 %collective-permute-start.83 = (f32[1,4,1,64]{3,2,1,0:T(1,128)S(1)}, f32[1,4,1,64]{3,2,1,0:T(1,128)S(1)}, u32[]{:S(2)}, u32[]{:S(2)}) collective-permute-start(f32[1,4,1,64]{3,2,1,0:T(1,128)S(1)} %get-tuple-element.157), channel_id=1, source_target_pairs={{1,0},{2,1},{3,2},{4,3},{5,4},{6,5},{7,6},{8,7},{9,8},{10,9},{11,1... | collective-permute-start | bytes 3080 | tf_op jit(solution)/shard_map/ppermute | solution.py:25
  841.4 9.7 collective-permute-start.42
  856.2 13.3 %collective-permute-start.44 = (f32[1,1,4,128]{3,2,1,0:T(4,128)S(1)}, f32[1,1,4,128]{3,2,1,0:T(4,128)S(1)}, u32[]{:S(2)}, u32[]{:S(2)}) collective-permute-start(f32[1,1,4,128]{3,2,1,0:T(4,128)S(1)} %get-tuple-element.144), channel_id=1, source_target_pairs={{0,32},{32,64},{64,96},{96,128},{128,160},{160,192},{192,224},{224... | collective-permute-start | bytes 6152 | tf_op jit(solution)/shard_map/ppermute | solution.py:23
  862.9 12.0 %collective-permute-start.84 = (f32[1,1,4,128]{3,2,1,0:T(4,128)S(1)}, f32[1,1,4,128]{3,2,1,0:T(4,128)S(1)}, u32[]{:S(2)}, u32[]{:S(2)}) collective-permute-start(f32[1,1,4,128]{3,2,1,0:T(4,128)S(1)} %get-tuple-element.140), channel_id=1, source_target_pairs={{0,32},{32,64},{64,96},{96,128},{128,160},{160,192},{192,224},{224... | collective-permute-start | bytes 6152 | tf_op jit(solution)/shard_map/ppermute | solution.py:23
  869.5 13.1 %collective-permute-start.46 = (f32[1,6,1,128]{3,2,1,0:T(1,128)S(1)}, f32[1,6,1,128]{3,2,1,0:T(1,128)S(1)}, u32[]{:S(2)}, u32[]{:S(2)}) collective-permute-start(f32[1,6,1,128]{3,2,1,0:T(1,128)S(1)} %get-tuple-element.126), channel_id=1, source_target_pairs={{0,1},{1,2},{2,3},{3,4},{4,5},{5,6},{6,7},{7,8},{8,9},{9,10},{10,1... | collective-permute-start | bytes 9224 | tf_op jit(solution)/shard_map/ppermute | solution.py:23
  873.0 9.7 collective-permute-start.47
  874.9 15.5 %collective-permute-start.86 = (f32[1,6,1,128]{3,2,1,0:T(1,128)S(1)}, f32[1,6,1,128]{3,2,1,0:T(1,128)S(1)}, u32[]{:S(2)}, u32[]{:S(2)}) collective-permute-start(f32[1,6,1,128]{3,2,1,0:T(1,128)S(1)} %get-tuple-element.122), channel_id=1, source_target_pairs={{0,1},{1,2},{2,3},{3,4},{4,5},{5,6},{6,7},{7,8},{8,9},{9,10},{10,1... | collective-permute-start | bytes 9224 | tf_op jit(solution)/shard_map/ppermute | solution.py:23
  880.7 9.7 %collective-permute-start.87 = (f32[1,6,1,128]{3,2,1,0:T(1,128)S(1)}, f32[1,6,1,128]{3,2,1,0:T(1,128)S(1)}, u32[]{:S(2)}, u32[]{:S(2)}) collective-permute-start(f32[1,6,1,128]{3,2,1,0:T(1,128)S(1)} %get-tuple-element.123), channel_id=1, source_target_pairs={{1,0},{2,1},{3,2},{4,3},{5,4},{6,5},{7,6},{8,7},{9,8},{10,9},{11,1... | collective-permute-start | bytes 9224 | tf_op jit(solution)/shard_map/ppermute | solution.py:25
  894.0 10.0 %collective-permute-start.50 = (f32[1,6,1,128]{3,2,1,0:T(1,128)S(1)}, f32[1,6,1,128]{3,2,1,0:T(1,128)S(1)}, u32[]{:S(2)}, u32[]{:S(2)}) collective-permute-start(f32[1,6,1,128]{3,2,1,0:T(1,128)S(1)} %get-tuple-element.124), channel_id=1, source_target_pairs={{0,1},{1,2},{2,3},{3,4},{4,5},{5,6},{6,7},{7,8},{8,9},{9,10},{10,1... | collective-permute-start | bytes 9224 | tf_op jit(solution)/shard_map/ppermute | solution.py:23
  910.0 10.6 %collective-permute-start.52 = (f32[1,1,8,256]{3,2,1,0:T(8,128)S(1)}, f32[1,1,8,256]{3,2,1,0:T(8,128)S(1)}, u32[]{:S(2)}, u32[]{:S(2)}) collective-permute-start(f32[1,1,8,256]{3,2,1,0:T(8,128)S(1)} %get-tuple-element.112), channel_id=1, source_target_pairs={{0,32},{32,64},{64,96},{96,128},{128,160},{160,192},{192,224},{224... | collective-permute-start | bytes 24584 | tf_op jit(solution)/shard_map/ppermute | solution.py:23
  915.3 10.4 %collective-permute-start.88 = (f32[1,1,4,128]{3,2,1,0:T(4,128)S(1)}, f32[1,1,4,128]{3,2,1,0:T(4,128)S(1)}, u32[]{:S(2)}, u32[]{:S(2)}) collective-permute-start(f32[1,1,4,128]{3,2,1,0:T(4,128)S(1)} %get-tuple-element.138), channel_id=1, source_target_pairs={{0,32},{32,64},{64,96},{96,128},{128,160},{160,192},{192,224},{224... | collective-permute-start | bytes 6152 | tf_op jit(solution)/shard_map/ppermute | solution.py:23
  920.6 12.7 %collective-permute-start.54 = (f32[1,10,1,256]{3,2,1,0:T(1,128)S(1)}, f32[1,10,1,256]{3,2,1,0:T(1,128)S(1)}, u32[]{:S(2)}, u32[]{:S(2)}) collective-permute-start(f32[1,10,1,256]{3,2,1,0:T(1,128)S(1)} %get-tuple-element.102), channel_id=1, source_target_pairs={{0,1},{1,2},{2,3},{3,4},{4,5},{5,6},{6,7},{7,8},{8,9},{9,10},{10,1... | collective-permute-start | bytes 30728 | tf_op jit(solution)/shard_map/ppermute | solution.py:23
  923.7 9.7 collective-permute-start.55
  925.7 14.9 %collective-permute-start.90 = (f32[1,6,1,128]{3,2,1,0:T(1,128)S(1)}, f32[1,6,1,128]{3,2,1,0:T(1,128)S(1)}, u32[]{:S(2)}, u32[]{:S(2)}) collective-permute-start(f32[1,6,1,128]{3,2,1,0:T(1,128)S(1)} %get-tuple-element.120), channel_id=1, source_target_pairs={{0,1},{1,2},{2,3},{3,4},{4,5},{5,6},{6,7},{7,8},{8,9},{9,10},{10,1... | collective-permute-start | bytes 9224 | tf_op jit(solution)/shard_map/ppermute | solution.py:23
  944.3 10.6 %collective-permute-start.58 = (f32[1,10,1,256]{3,2,1,0:T(1,128)S(1)}, f32[1,10,1,256]{3,2,1,0:T(1,128)S(1)}, u32[]{:S(2)}, u32[]{:S(2)}) collective-permute-start(f32[1,10,1,256]{3,2,1,0:T(1,128)S(1)} %get-tuple-element.100), channel_id=1, source_target_pairs={{0,1},{1,2},{2,3},{3,4},{4,5},{5,6},{6,7},{7,8},{8,9},{9,10},{10,1... | collective-permute-start | bytes 30728 | tf_op jit(solution)/shard_map/ppermute | solution.py:23
  (83 other events, 4670.3 us)
Sparse Core Ops, SparseCore 0:
  254.3 449.0 all-reduce.45
where the time goes:
time: 972 us; the launch traced here: 967 us
  waiting for transfers between devices  516 us (53%)
  starting transfers between devices  299 us (31%)
  other arithmetic  68.6 us (7%)
  between operations  55.9 us (6%)
  local copies, waits for them, and re-layouts  27.2 us (3%)
    unnamed x2, waiting for transfers between devices  449 us
    ppermute x46, starting transfers between devices, with_halo(): lax.ppermute(tail, axis, [(i, (i + 1) % count) for i in range(ends)])  203 us
    ppermute x46, starting transfers between devices, with_halo(): lax.ppermute(head, axis, [((i + 1) % count, i) for i in range(ends)])  96.3 us
    ppermute x46, waiting for transfers between devices, with_halo(): lax.ppermute(head, axis, [((i + 1) % count, i) for i in range(ends)])  66.8 us
    reduce_sum x27, other arithmetic, inner(): return jnp.sum(left * right, axis=(-3, -2, -1), keepdims=True)  36 us
  transfers between devices with their start and end apart: 93, of which 18 were waited for; matrix products, arithmetic and copies ran while one was open for 3% of the time, Pallas kernels for 0%

commit v1 on v0

v1 whole, which is shorter than its diff:
```python
import jax
import jax.numpy as jnp
from jax import lax
from jax.experimental import pallas as pl
from jax.experimental.pallas import tpu as pltpu
from jax.sharding import PartitionSpec as P


CSWEEPS = 8
OMEGA = 0.8
F32 = jnp.float32
ROWS = 16

INNER = [(dx, dy) for dx in (-1, 1, 0) for dy in (0, -1, 1) if (dx, dy) != (0, 0)]
AROUND = INNER + [
    (dx, dy) for dx in (-2, 2, -1, 1, 0) for dy in (-2, -1, 0, 1, 2) if max(abs(dx), abs(dy)) == 2
]

(G_K0, G_S0, G_E1, G_K2, G_ZK, G_GK, G_B1, G_B2, G_ZB, G_GB, G_V0, G_V1, G_U2) = range(13)
GROUPS = 13


def span(step, size, rim):
    low = max(0, step * size - rim)
    high = min(size, size + rim + step * size)
    return low, high - low, low - step * size


def roll(x, shift, axis):
    return pltpu.roll(x, shift % x.shape[axis], axis)


def iota(shape, axis):
    return lax.broadcasted_iota(jnp.int32, shape, axis)


def take_lanes(x, index):
    return jnp.take_along_axis(x, index, axis=1)


def take_rows(x, index):
    return jnp.take_along_axis(x, index, axis=0)


def pair_lanes(a, b):
    lane = iota(a.shape, 1)
    index = lax.rem(2 * lane, 128)
    a = take_lanes(a + roll(a, -1, 1), index)
    if b is None:
        return a
    b = take_lanes(b + roll(b, -1, 1), index)
    return jnp.where(lane < 64, a, b)


def pair_rows(x):
    return take_rows(x + roll(x, -1, 0), lax.rem(2 * iota(x.shape, 0), 8))


def kernel(nx, ny, src_hbm, kap_hbm, fine_ref, coarse_ref, K0, S0, V0, VA0, VB0, C0, E1, B1, V1, VA1, VB1, C1, M1,
           K2, B2, U2, VA2, VB2, C2, M2, ZK, ZB, GK, GB, C3, R3, W3, P3, Q3, X3, S5, T5, D, local_sem, send_sem, recv_sem):
    gx = lax.axis_index("gx")
    gy = lax.axis_index("gy")
    mesh_ids = pl.DeviceIdType.MESH

    def peer(dx, dy):
        return (lax.rem(gx + (dx + nx), nx) if not isinstance(dx, int) or dx else gx,
                lax.rem(gy + (dy + ny), ny) if not isinstance(dy, int) or dy else gy)

    sent = [0]

    def wait_rows(rows, sem):
        pltpu.make_async_copy(D.at[pl.ds(0, rows)], D.at[pl.ds(0, rows)], sem).wait()

    def wait_group(group, rows):
        wait_rows(rows, recv_sem.at[group])

    def ship(group, ref, lead, steps, size, rim, corner, offset):
        total = 0
        for dx, dy in steps:
            reach = corner if dx and dy else rim
            px, cx, qx = span(dx, size, reach)
            py, cy, qy = span(dy, size, reach)
            here = (pl.ds(px + offset, cx), pl.ds(py, cy), slice(None))
            there = (pl.ds(qx + offset, cx), pl.ds(qy % ROWS, cy), slice(None))
            if lead is not None:
                here, there = (pl.ds(*lead),) + here, (pl.ds(*lead),) + there
            pltpu.make_async_remote_copy(
                src_ref=ref.at[here], dst_ref=ref.at[there], send_sem=send_sem.at[group], recv_sem=recv_sem.at[group],
                device_id=peer(dx, dy), device_id_type=mesh_ids,
            ).start()
            total += cx * cy * (ref.shape[-1] // 128) * (lead[1] if lead else 1)
        return total

    def ship_column(group, ref):
        def step(i, carry):
            pltpu.make_async_remote_copy(
                src_ref=ref.at[pl.ds(gx, 1)], dst_ref=ref.at[pl.ds(gx, 1)], send_sem=send_sem.at[group],
                recv_sem=recv_sem.at[group], device_id=(lax.rem(gx + i, nx), gy), device_id_type=mesh_ids,
            ).start()
            return carry
        lax.fori_loop(1, nx, step, 0)
        return nx - 1

    def ship_row(group, ref):
        def step(i, carry):
            pltpu.make_async_remote_copy(
                src_ref=ref.at[gy], dst_ref=ref.at[gy], send_sem=send_sem.at[group],
                recv_sem=recv_sem.at[group], device_id=(gx, lax.rem(gy + i, ny)), device_id_type=mesh_ids,
            ).start()
            return carry
        lax.fori_loop(1, ny, step, 0)
        return 8 * (ny - 1)

    copies = [
        pltpu.make_async_copy(kap_hbm, K0.at[pl.ds(3, 8), pl.ds(0, 8), :], local_sem.at[0]),
        pltpu.make_async_copy(src_hbm, S0.at[pl.ds(2, 8), pl.ds(0, 8), :], local_sem.at[1]),
    ]
    for copy in copies:
        copy.start()
    barrier = pltpu.get_barrier_semaphore()

    def greet(device):
        pl.semaphore_signal(barrier, inc=1, device_id=device, device_id_type=mesh_ids)

    def greet_x(i, carry):
        greet((lax.rem(gx + i, nx), gy))
        return carry

    def greet_y(i, carry):
        greet((gx, lax.rem(gy + i, ny)))
        return carry

    lax.fori_loop(1, nx, greet_x, 0)
    lax.fori_loop(1, ny, greet_y, 0)
    diagonal = [(dx, dy) for dx, dy in AROUND if dx and dy]
    for dx, dy in diagonal:
        greet(peer(dx, dy))
    for copy in copies:
        copy.wait()
    pl.semaphore_wait(barrier, nx - 1 + ny - 1 + len(diagonal))

    n_k0 = ship(G_K0, K0, None, INNER, 8, 3, 2, 3)
    n_s0 = ship(G_S0, S0, None, INNER, 8, 2, 1, 2)

    def restrict0(ref, offset, scale):
        out = []
        for i in range(4):
            both = ref[offset + 2 * i, 0:8, :] + ref[offset + 2 * i + 1, 0:8, :]
            out.append(scale * pair_rows(pair_lanes(both[:, :128], both[:, 128:])))
        return out

    own1 = restrict0(K0, 3, 0.125)
    for i, tile in enumerate(own1):
        E1[1, 3 + i, 0:4, :] = tile[0:4]
    for i, tile in enumerate(restrict0(S0, 2, 0.5)):
        E1[0, 3 + i, 0:4, :] = tile[0:4]
    n_e1 = ship(G_E1, E1, (0, 2), INNER, 4, 3, 3, 3)
    own2 = []
    for i in range(2):
        own2.append(0.125 * pair_rows(pair_lanes(own1[2 * i] + own1[2 * i + 1], None)))
        K2[4 + i, 0:2, :] = own2[i][0:2]
    n_k2 = ship(G_K2, K2, None, AROUND, 2, 4, 4, 4)
    both = own2[0] + own2[1]
    ZK[pl.ds(gx, 1), :] = 0.125 * pair_rows(pair_lanes(both, None))[0:1]
    n_zk = ship_column(G_ZK, ZK)

    def inside(shape, first, size, rim):
        plane = iota(shape, 0) + first + gx * size
        row = iota(shape, 1)
        row = jnp.where(row < 8 + size // 2, row, row - ROWS)
        good = (row >= -rim) & (row < size + rim)
        row = row + gy * size
        return good & (plane >= 0) & (plane < nx * size) & (row >= 0) & (row < ny * size)

    def faces(read, C, planes, width, depth, size, rim, first, chunk):
        for a in range(0, planes, chunk):
            n = min(chunk, planes - a)
            k = read(a, n + 2)
            mid = k[1:n + 1]
            west = 0.5 * (k[0:n + 1] + k[1:n + 2])
            C[0, a:a + n + 1] = west
            north = 0.5 * (mid + roll(mid, -1, 1))
            south = roll(north, 1, 1)
            z = lax.rem(iota(mid.shape, 2), depth)
            top = z == depth - 1
            bottom = z == 0
            above = 0.5 * (mid + jnp.where(top, 0.0, roll(mid, -1, 2)))
            below = 0.5 * (mid + jnp.where(bottom, 0.0, roll(mid, 1, 2)))
            total = west[0:n] + west[1:n + 1] + north + south + above + below
            C[1, a:a + n] = north
            C[2, a:a + n] = south
            C[3, a:a + n] = jnp.where(top, 0.0, above)
            C[4, a:a + n] = jnp.where(bottom, 0.0, below)
            C[5, a:a + n] = total
            C[6, a:a + n] = jnp.where(inside(mid.shape, first + a, size, rim), OMEGA / total, 0.0)

    def residual(v, b, C, c, n, rows=ROWS):
        mid = v[1:n + 1]
        cut = slice(0, rows)
        beside = C[0, c:c + n, cut] * v[0:n, cut] + C[0, c + 1:c + n + 1, cut] * v[2:n + 2, cut]
        beside += C[1, c:c + n, cut] * roll(mid, -1, 1)[:, cut] + C[2, c:c + n, cut] * roll(mid, 1, 1)[:, cut]
        mid = mid[:, cut]
        beside += C[3, c:c + n, cut] * roll(mid, -1, 2) + C[4, c:c + n, cut] * roll(mid, 1, 2)
        return b - C[5, c:c + n, cut] * mid + beside

    def sweep(V, vo, b, C, co, store, first, planes, chunk, rows=ROWS):
        for a in range(0, planes, chunk):
            n = min(chunk, planes - a)
            p = first + a
            v = V(p - 1, n + 2)
            r = residual(v, b(p, n, rows), C, p + co, n, rows)
            store(p, n, v[1:n + 1, 0:rows] + C[6, p + co:p + co + n, 0:rows] * r)

    wait_group(G_K0, n_k0)

    def read_k0(a, n):
        k = K0[a:a + n]
        return jnp.where(inside(k.shape, a - 3, 8, 3), k, 0.0)

    faces(read_k0, C0, 12, 256, 256, 8, 3, -2, 2)
    wait_group(G_S0, n_s0)
    for a in range(0, 12, 2):
        VA0[a:a + 2] = C0[6, a:a + 2] * S0[a:a + 2]

    def at(ref, offset, lead=None):
        def read(p, n, rows=ROWS):
            where = (pl.ds(p + offset, n), pl.ds(0, rows), slice(None))
            return ref[where] if lead is None else ref[(lead,) + where]
        return read

    def to(ref, offset, lead=None):
        def store(p, n, x):
            where = (pl.ds(p + offset, n), pl.ds(0, x.shape[1]), slice(None))
            if lead is None:
                ref[where] = x
            else:
                ref[(lead,) + where] = x
        return store

    sweep(at(VA0, 2), 2, at(S0, 2), C0, 2, to(VB0, 1), -1, 10, 2)
    for i in range(4):
        r = residual(VB0[2 * i:2 * i + 4], S0[2 + 2 * i:4 + 2 * i, 0:8], C0, 2 + 2 * i, 2, 8)
        both = r[0] + r[1]
        B1[3 + i, 0:4, :] = 0.5 * pair_rows(pair_lanes(both[:, :128], both[:, 128:]))[0:4]
    n_b1 = ship(G_B1, B1, None, INNER, 4, 2, 2, 3)
    V0[2:10, 0:8, :] = VB0[1:9, 0:8, :]

    wait_group(G_ZK, n_zk)

    def packed(ref):
        keep = lax.rem(iota((8, 128), 0) + 8 * (iota((8, 128), 1) // 64), 16) < nx
        return jnp.where(keep, jnp.where(iota((8, 128), 1) < 64, ref[0:8], ref[8:16]), 0.0)

    GK[gy] = packed(ZK)
    n_gk = ship_row(G_GK, GK)
    wait_group(G_E1, n_e1)

    def read_k1(a, n):
        k = E1[1, a:a + n]
        return jnp.where(inside(k.shape, a - 3, 4, 3), k, 0.0)

    faces(read_k1, C1, 8, 128, 128, 4, 3, -2, 4)
    b1 = (at(B1, 3), at(E1, 3, 0))

    def down1(k):
        for a in range(0, 8, 4):
            VA1[k, a:a + 4] = C1[6, a:a + 4] * b1[k](a - 2, 4)
        sweep(at(VA1, 2, k), 2, b1[k], C1, 2, to(VB1, 1, k), -1, 6, 6)
        r = residual(VB1[k], b1[k](0, 4, 8), C1, 2, 4, 8)
        V1[k, 3:7, 0:4, :] = VB1[k, 1:5, 0:4, :]
        return r[0] + r[1], r[2] + r[3]

    pairs_c = down1(1)
    wait_group(G_B1, n_b1)
    pairs_f = down1(0)
    for i in range(2):
        tile = 0.5 * pair_rows(pair_lanes(pairs_f[i], pairs_c[i]))
        B2[2 + i, 0:2, :] = tile[0:2]
        U2[0, 4 + i, 0:2, :] = tile[0:2]
    n_b2 = ship(G_B2, B2, None, INNER, 2, 2, 2, 2)

    wait_group(G_K2, n_k2)

    def read_k2(a, n):
        k = K2[a:a + n]
        return jnp.where(inside(k.shape, a - 4, 2, 4), k, 0.0)

    faces(read_k2, C2, 8, 128, 64, 2, 4, -3, 4)
    wait_group(G_B2, n_b2)
    VA2[0:6] = C2[6, 1:7] * B2[0:6]
    sweep(at(VA2, 2), 2, at(B2, 2), C2, 3, to(VB2, 1), -1, 4, 4)
    r = residual(VB2[0:4], B2[2:4, 0:8], C2, 3, 2, 8)
    U2[1, 4:6, 0:2, :] = VB2[1:3, 0:2, :]
    ZB[pl.ds(gx, 1), :] = 0.5 * pair_rows(pair_lanes(r[0] + r[1], None))[0:1]
    n_zb = ship_column(G_ZB, ZB)

    shape = (8, 128)
    sub, lane = iota(shape, 0), iota(shape, 1)
    half = lane // 64
    at_x = sub + 8 * half
    z = lax.rem(lane, 32)
    first_rhs = lax.rem(lane, 64) < 32

    def next_x(v):
        a = roll(v, -1, 1)
        return jnp.where(sub == 7, roll(a, 64, 2), a)

    def previous_x(v):
        a = roll(v, 1, 1)
        return jnp.where(sub == 0, roll(a, 64, 2), a)

    wait_group(G_GK, n_gk)
    chunk3 = min(8, ny)
    blank = jnp.zeros(shape, F32)
    for a in range(0, ny, chunk3):
        k = GK[a:a + chunk3]
        up_y = [GK[j] if j < ny else blank for j in range(a + 1, a + chunk3 + 1)]
        down_y = [GK[j] if j >= 0 else blank for j in range(a - 1, a + chunk3 - 1)]
        y_next = 0.5 * (k + jnp.stack(up_y))
        y_previous = 0.5 * (k + jnp.stack(down_y))
        x_next = 0.5 * (k + jnp.where(at_x < nx - 1, next_x(k), 0.0))
        x_previous = 0.5 * (k + jnp.where(at_x > 0, previous_x(k), 0.0))
        z_next = 0.5 * (k + jnp.where(z < 31, roll(k, -1, 2), 0.0))
        z_previous = 0.5 * (k + jnp.where(z > 0, roll(k, 1, 2), 0.0))
        C3[0, a:a + chunk3] = y_previous
        C3[1, a:a + chunk3] = y_next
        C3[2, a:a + chunk3] = jnp.where(at_x < nx - 1, x_next, 0.0)
        C3[3, a:a + chunk3] = jnp.where((at_x > 0) & (at_x < nx), x_previous, 0.0)
        C3[4, a:a + chunk3] = jnp.where(z < 31, z_next, 0.0)
        C3[5, a:a + chunk3] = jnp.where(z > 0, z_previous, 0.0)
        C3[6, a:a + chunk3] = y_next + y_previous + x_next + x_previous + z_next + z_previous
    R3[0] = blank
    R3[ny + 1] = blank

    wait_group(G_ZB, n_zb)
    GB[gy] = packed(ZB)
    n_gb = ship_row(G_GB, GB)
    n_v0 = ship(G_V0, V0, None, INNER, 8, 2, 1, 2)
    n_v1 = ship(G_V1, V1, (0, 2), INNER, 4, 3, 3, 3)
    n_u2 = ship(G_U2, U2, (0, 2), AROUND, 2, 4, 4, 4)
    for a in range(0, ny, chunk3):
        P3[a:a + chunk3] = jnp.zeros((chunk3,) + shape, F32)
        Q3[a:a + chunk3] = jnp.zeros((chunk3,) + shape, F32)
        X3[2 + a:2 + a + chunk3] = jnp.zeros((chunk3,) + shape, F32)
    wait_group(G_GB, n_gb)
    for a in range(0, ny, chunk3):
        R3[1 + a:1 + a + chunk3] = GB[a:a + chunk3]

    def over_grid(x):
        x = jnp.sum(x, axis=0, keepdims=True)
        first = jnp.sum(jnp.where(first_rhs[0:1], x, 0.0), axis=1, keepdims=True)
        second = jnp.sum(jnp.where(first_rhs[0:1], 0.0, x), axis=1, keepdims=True)
        return jnp.where(first_rhs[0:1], first, second)

    def iteration(_, carry):
        norm_before, alpha_before = carry
        norm, energy = blank, blank
        for a in range(0, ny, chunk3):
            mid = R3[1 + a:1 + a + chunk3]
            beside = C3[0, a:a + chunk3] * R3[a:a + chunk3] + C3[1, a:a + chunk3] * R3[2 + a:2 + a + chunk3]
            beside += C3[2, a:a + chunk3] * next_x(mid) + C3[3, a:a + chunk3] * previous_x(mid)
            beside += C3[4, a:a + chunk3] * roll(mid, -1, 2) + C3[5, a:a + chunk3] * roll(mid, 1, 2)
            image = C3[6, a:a + chunk3] * mid - beside
            W3[a:a + chunk3] = image
            norm += jnp.sum(mid * mid, axis=0)
            energy += jnp.sum(mid * image, axis=0)
        norm, energy = over_grid(norm), over_grid(energy)
        beta = norm / norm_before
        alpha = norm / (energy - beta * norm / alpha_before)
        for a in range(0, ny, chunk3):
            p = R3[1 + a:1 + a + chunk3] + beta * P3[a:a + chunk3]
            q = W3[a:a + chunk3] + beta * Q3[a:a + chunk3]
            P3[a:a + chunk3] = p
            Q3[a:a + chunk3] = q
            X3[2 + a:2 + a + chunk3] += alpha * p
            R3[1 + a:1 + a + chunk3] -= alpha * q
        return norm, alpha

    lax.fori_loop(0, CSWEEPS, iteration, (jnp.full((1, 128), jnp.inf, F32), jnp.ones((1, 128), F32)))

    near = X3[pl.ds(gy, 5)]
    S5[:, 2:10, :] = near
    S5[:, 10:18, :] = roll(near, 64, 2)
    for dx in range(-2, 3):
        for dy in range(-2, 3):
            T5[dx + 2, pl.ds(dy % ROWS, 1), :] = S5[dy + 2, pl.ds(gx + (dx + 2), 1), :]

    lane2 = lane // 2
    row_low, row_high = sub // 2, 4 + sub // 2

    wait_group(G_U2, n_u2)
    for i in range(5):
        low = take_rows(take_lanes(T5[i, 0:8], lane2), row_low)
        high = take_rows(take_lanes(T5[i, 8:16], lane2), row_high)
        for p in (2 * i, 2 * i + 1):
            v = U2[1, p] + jnp.concatenate([low, high], axis=0)
            M2[p:p + 1] = jnp.where(inside((1, ROWS, 128), p - 4, 2, 4), v[None], 0.0)
    sweep(at(M2, 4), 4, at(U2, 4, 0), C2, 3, to(VA2, 3), -3, 8, 4)
    sweep(at(VA2, 3), 3, at(U2, 4, 0), C2, 3, to(VB2, 2), -2, 6, 6)

    wait_group(G_V1, n_v1)
    for p1 in range(-3, 7):
        e = VB2[p1 // 2 + 2]
        good = inside((1, ROWS, 128), p1, 4, 3)
        for k in range(2):
            index = lane2 + 64 * k
            low = take_rows(take_lanes(e[0:8], index), row_low)
            high = take_rows(take_lanes(e[8:16], index), row_high)
            v = V1[k, p1 + 3] + jnp.concatenate([low, high], axis=0)
            M1[k, p1 + 3:p1 + 4] = jnp.where(good, v[None], 0.0)
    for k in range(2):
        sweep(at(M1, 3, k), 3, b1[k], C1, 2, to(VA1, 2, k), -2, 8, 4)
    sweep(at(VA1, 2, 0), 2, b1[0], C1, 2, to(VB1, 1, 0), -1, 6, 6)

    def store_coarse(p, n, x):
        coarse_ref[pl.ds(p, n)] = x[:, 0:4]

    sweep(at(VA1, 2, 1), 2, b1[1], C1, 2, store_coarse, 0, 4, 4, 8)

    wait_group(G_V0, n_v0)
    for p1 in range(-1, 5):
        e = VB1[0, p1 + 1]
        pieces = []
        for k in range(2):
            index = lane2 + 64 * k
            first, second = take_lanes(e[0:8], index), take_lanes(e[8:16], index)
            low = take_rows(first, row_low)
            high = jnp.where(sub < 4, take_rows(first, row_high), take_rows(second, row_high))
            pieces.append(jnp.concatenate([low, high], axis=0))
        e = jnp.concatenate(pieces, axis=1)
        v = V0[2 * p1 + 2:2 * p1 + 4] + e[None]
        VA0[2 * p1 + 2:2 * p1 + 4] = jnp.where(inside(v.shape, 2 * p1, 8, 2), v, 0.0)
    sweep(at(VA0, 2), 2, at(S0, 2), C0, 2, to(VB0, 1), -1, 10, 2)
    sweep(at(VB0, 1), 1, at(S0, 2), C0, 2, to(fine_ref, 0), 0, 8, 2, 8)

    for group, rows in ((G_K0, n_k0), (G_S0, n_s0), (G_E1, n_e1), (G_K2, n_k2), (G_ZK, n_zk), (G_GK, n_gk), (G_B1, n_b1),
                        (G_B2, n_b2), (G_ZB, n_zb), (G_GB, n_gb), (G_V0, n_v0), (G_V1, n_v1), (G_U2, n_u2)):
        wait_rows(rows, send_sem.at[group])


def solution(mesh):
    nx, ny = mesh.shape["gx"], mesh.shape["gy"]

    def vmem(*shape):
        return pltpu.VMEM(shape, F32)

    def on_device(source, kappa):
        scratch = [
            vmem(14, 16, 256), vmem(12, 16, 256), vmem(12, 16, 256), vmem(12, 16, 256), vmem(10, 16, 256),
            vmem(7, 13, 16, 256),
            vmem(2, 10, 16, 128), vmem(10, 16, 128), vmem(2, 10, 16, 128), vmem(2, 8, 16, 128), vmem(2, 6, 16, 128),
            vmem(7, 9, 16, 128), vmem(2, 10, 16, 128),
            vmem(10, 16, 128), vmem(6, 16, 128), vmem(2, 10, 16, 128), vmem(8, 16, 128), vmem(6, 16, 128),
            vmem(7, 9, 16, 128), vmem(10, 16, 128),
            vmem(16, 128), vmem(16, 128), vmem(ny, 8, 128), vmem(ny, 8, 128),
            vmem(7, ny, 8, 128), vmem(ny + 2, 8, 128), vmem(ny, 8, 128), vmem(ny, 8, 128), vmem(ny, 8, 128),
            vmem(ny + 4, 8, 128), vmem(5, 24, 128), vmem(5, 16, 128),
            vmem(512, 128),
            pltpu.SemaphoreType.DMA((2,)), pltpu.SemaphoreType.DMA((GROUPS,)), pltpu.SemaphoreType.DMA((GROUPS,)),
        ]
        return pl.pallas_call(
            lambda *refs: kernel(nx, ny, *refs),
            out_shape=(jax.ShapeDtypeStruct((8, 8, 256), F32), jax.ShapeDtypeStruct((4, 4, 128), F32)),
            in_specs=[pl.BlockSpec(memory_space=pl.ANY)] * 2,
            out_specs=[pl.BlockSpec(memory_space=pltpu.VMEM)] * 2,
            scratch_shapes=scratch,
            compiler_params=pltpu.CompilerParams(
                collective_id=0, has_side_effects=True, vmem_limit_bytes=32 * 1024 * 1024
            ),
            name="vcycles",
        )(source, kappa)

    spec = P("gx", "gy", None)
    return jax.shard_map(on_device, mesh=mesh, in_specs=(spec, spec), out_specs=(spec, spec), check_vma=False)
```

time: 972 us -> 51.8 us (0.05)
  the two profiles are of different devices: /device:TPU:103 before, /device:TPU:1 now
where the time goes in v1:
time: 51.8 us; the launch traced here: 51.6 us
  Pallas kernels  48 us (93%)
  local copies, waits for them, and re-layouts  2.9 us (6%)
  between operations  0.65 us (1%)
    pallas_call x1, Pallas kernels, on_device(): pl.pallas_call(lambda *refs: kernel(nx, ny, *refs), out_shape=(jax.ShapeD...  48 us
    unnamed x6, local copies, waits for them, and re-layouts  2.9 us

profile of v1, /device:TPU:1, one launch (start us, length us, event | category | flops | bytes accessed | tf_op | source)
XLA Modules:
  0.0 51.6 jit_solution(5985816369416332625)
XLA Ops:
  0.6 0.0 copy-start
  0.6 0.8 %copy-done = f32[8,8,256]{2,1,0:T(8,128)S(1)} copy-done((f32[8,8,256]{2,1,0:T(8,128)S(1)}, f32[8,8,256]{2,1,0:T(8,128)}, u32[]{:S(2)}) %copy-start) | copy-done | bytes 65560
  1.5 0.0 copy-start.1
  1.5 0.8 %copy-done.1 = f32[8,8,256]{2,1,0:T(8,128)S(1)} copy-done((f32[8,8,256]{2,1,0:T(8,128)S(1)}, f32[8,8,256]{2,1,0:T(8,128)}, u32[]{:S(2)}) %copy-start.1) | copy-done | bytes 65560
  2.3 48.0 %vcycles.1 = (f32[8,8,256]{2,1,0:T(8,128)S(1)}, f32[4,4,128]{2,1,0:T(4,128)S(1)}) custom-call(f32[8,8,256]{2,1,0:T(8,128)S(1)} %copy-done, f32[8,8,256]{2,1,0:T(8,128)S(1)} %copy-done.1), custom_call_target="tpu_custom_call" | custom-call | tf_op jit(solution)/shard_map/vcycles/pallas_call | solution.py:461
  50.3 0.6 %copy.6 = f32[8,8,256]{2,1,0:T(8,128)} copy(f32[8,8,256]{2,1,0:T(8,128)S(1)} %get-tuple-element.4) | data formatting | bytes 131072
  51.0 0.6 %copy.7 = f32[4,4,128]{2,1,0:T(4,128)} copy(f32[4,4,128]{2,1,0:T(4,128)S(1)} %get-tuple-element.5) | data formatting | bytes 16384
Async XLA Ops:
  0.6 0.8 %copy-start = (f32[8,8,256]{2,1,0:T(8,128)S(1)}, f32[8,8,256]{2,1,0:T(8,128)}, u32[]{:S(2)}) copy-start(f32[8,8,256]{2,1,0:T(8,128)} %refs_0_.1) | copy-start | bytes 196612
  1.5 0.8 %copy-start.1 = (f32[8,8,256]{2,1,0:T(8,128)S(1)}, f32[8,8,256]{2,1,0:T(8,128)}, u32[]{:S(2)}) copy-start(f32[8,8,256]{2,1,0:T(8,128)} %refs_1_.1) | copy-start | bytes 196612

commit v2 on v1

--- a/solution.py
+++ b/solution.py
@@ -8,6 +8,7 @@
 
 CSWEEPS = 8
 OMEGA = 0.8
+REACH = 4
 F32 = jnp.float32
 ROWS = 16
 
@@ -57,7 +58,7 @@
 
 
 def kernel(nx, ny, src_hbm, kap_hbm, fine_ref, coarse_ref, K0, S0, V0, VA0, VB0, C0, E1, B1, V1, VA1, VB1, C1, M1,
-           K2, B2, U2, VA2, VB2, C2, M2, ZK, ZB, GK, GB, C3, R3, W3, P3, Q3, X3, S5, T5, D, local_sem, send_sem, recv_sem):
+           K2, B2, U2, VA2, VB2, C2, M2, ZK, ZB, GK, GB, C3, R3, W3, P3, Q3, X3, S5, T5, D, local_sem, send_sem, recv_sem, word):
     gx = lax.axis_index("gx")
     gy = lax.axis_index("gy")
     mesh_ids = pl.DeviceIdType.MESH
@@ -65,8 +66,6 @@
     def peer(dx, dy):
         return (lax.rem(gx + (dx + nx), nx) if not isinstance(dx, int) or dx else gx,
                 lax.rem(gy + (dy + ny), ny) if not isinstance(dy, int) or dy else gy)
-
-    sent = [0]
 
     def wait_rows(rows, sem):
         pltpu.make_async_copy(D.at[pl.ds(0, rows)], D.at[pl.ds(0, rows)], sem).wait()
@@ -122,25 +121,26 @@
     def greet(device):
         pl.semaphore_signal(barrier, inc=1, device_id=device, device_id_type=mesh_ids)
 
-    def greet_x(i, carry):
-        greet((lax.rem(gx + i, nx), gy))
-        return carry
-
     def greet_y(i, carry):
         greet((gx, lax.rem(gy + i, ny)))
         return carry
 
-    lax.fori_loop(1, nx, greet_x, 0)
+    near = range(1, nx) if nx <= 2 * REACH else [*range(1, REACH + 1), *range(nx - REACH, nx)]
+    corners = [(dx, dy) for dx, dy in INNER if dx and dy]
+    for dx in near:
+        greet(peer(dx, 0))
+    for dx, dy in corners:
+        greet(peer(dx, dy))
     lax.fori_loop(1, ny, greet_y, 0)
-    diagonal = [(dx, dy) for dx, dy in AROUND if dx and dy]
-    for dx, dy in diagonal:
-        greet(peer(dx, dy))
+    pl.semaphore_wait(barrier, len(near) + ny - 1 + len(corners))
     for copy in copies:
         copy.wait()
-    pl.semaphore_wait(barrier, nx - 1 + ny - 1 + len(diagonal))
 
     n_k0 = ship(G_K0, K0, None, INNER, 8, 3, 2, 3)
     n_s0 = ship(G_S0, S0, None, INNER, 8, 2, 1, 2)
+    if nx > 2 * REACH:
+        for dx in (REACH, -REACH):
+            pl.semaphore_signal(word, inc=1, device_id=peer(dx, 0), device_id_type=mesh_ids)
 
     def restrict0(ref, offset, scale):
         out = []
@@ -159,10 +159,8 @@
     for i in range(2):
         own2.append(0.125 * pair_rows(pair_lanes(own1[2 * i] + own1[2 * i + 1], None)))
         K2[4 + i, 0:2, :] = own2[i][0:2]
-    n_k2 = ship(G_K2, K2, None, AROUND, 2, 4, 4, 4)
     both = own2[0] + own2[1]
     ZK[pl.ds(gx, 1), :] = 0.125 * pair_rows(pair_lanes(both, None))[0:1]
-    n_zk = ship_column(G_ZK, ZK)
 
     def inside(shape, first, size, rim):
         plane = iota(shape, 0) + first + gx * size
@@ -212,6 +210,7 @@
             store(p, n, v[1:n + 1, 0:rows] + C[6, p + co:p + co + n, 0:rows] * r)
 
     wait_group(G_K0, n_k0)
+    n_k2 = ship(G_K2, K2, None, AROUND, 2, 4, 4, 4)
 
     def read_k0(a, n):
         k = K0[a:a + n]
@@ -243,16 +242,16 @@
         both = r[0] + r[1]
         B1[3 + i, 0:4, :] = 0.5 * pair_rows(pair_lanes(both[:, :128], both[:, 128:]))[0:4]
     n_b1 = ship(G_B1, B1, None, INNER, 4, 2, 2, 3)
+    if nx > 2 * REACH:
+        pl.semaphore_wait(word, 2)
+    n_zk = ship_column(G_ZK, ZK)
     V0[2:10, 0:8, :] = VB0[1:9, 0:8, :]
 
-    wait_group(G_ZK, n_zk)
 
     def packed(ref):
         keep = lax.rem(iota((8, 128), 0) + 8 * (iota((8, 128), 1) // 64), 16) < nx
         return jnp.where(keep, jnp.where(iota((8, 128), 1) < 64, ref[0:8], ref[8:16]), 0.0)
 
-    GK[gy] = packed(ZK)
-    n_gk = ship_row(G_GK, GK)
     wait_group(G_E1, n_e1)
 
     def read_k1(a, n):
@@ -278,6 +277,9 @@
         B2[2 + i, 0:2, :] = tile[0:2]
         U2[0, 4 + i, 0:2, :] = tile[0:2]
     n_b2 = ship(G_B2, B2, None, INNER, 2, 2, 2, 2)
+    wait_group(G_ZK, n_zk)
+    GK[gy] = packed(ZK)
+    n_gk = ship_row(G_GK, GK)
 
     wait_group(G_K2, n_k2)
 
@@ -438,6 +440,17 @@
         wait_rows(rows, send_sem.at[group])
 
 
+def put_out(fine, coarse, fine_out, coarse_out, sem):
+    copies = [
+        pltpu.make_async_copy(fine, fine_out, sem.at[0]),
+        pltpu.make_async_copy(coarse, coarse_out, sem.at[1]),
+    ]
+    for copy in copies:
+        copy.start()
+    for copy in copies:
+        copy.wait()
+
+
 def solution(mesh):
     nx, ny = mesh.shape["gx"], mesh.shape["gy"]
 
@@ -456,19 +469,27 @@
             vmem(7, ny, 8, 128), vmem(ny + 2, 8, 128), vmem(ny, 8, 128), vmem(ny, 8, 128), vmem(ny, 8, 128),
             vmem(ny + 4, 8, 128), vmem(5, 24, 128), vmem(5, 16, 128),
             vmem(512, 128),
-            pltpu.SemaphoreType.DMA((2,)), pltpu.SemaphoreType.DMA((GROUPS,)), pltpu.SemaphoreType.DMA((GROUPS,)),
+            pltpu.SemaphoreType.DMA((2,)), pltpu.SemaphoreType.DMA((GROUPS,)), pltpu.SemaphoreType.DMA((GROUPS,)), pltpu.SemaphoreType.REGULAR,
         ]
-        return pl.pallas_call(
+        fine, coarse = pl.pallas_call(
             lambda *refs: kernel(nx, ny, *refs),
             out_shape=(jax.ShapeDtypeStruct((8, 8, 256), F32), jax.ShapeDtypeStruct((4, 4, 128), F32)),
-            in_specs=[pl.BlockSpec(memory_space=pl.ANY)] * 2,
+            in_specs=[pl.BlockSpec(memory_space=pltpu.HBM)] * 2,
             out_specs=[pl.BlockSpec(memory_space=pltpu.VMEM)] * 2,
             scratch_shapes=scratch,
             compiler_params=pltpu.CompilerParams(
                 collective_id=0, has_side_effects=True, vmem_limit_bytes=32 * 1024 * 1024
             ),
             name="vcycles",
-        )(source, kappa)
+        )(*(pltpu.with_memory_space_constraint(x, pltpu.HBM) for x in (source, kappa)))
+        return pl.pallas_call(
+            put_out,
+            out_shape=(jax.ShapeDtypeStruct((8, 8, 256), F32), jax.ShapeDtypeStruct((4, 4, 128), F32)),
+            in_specs=[pl.BlockSpec(memory_space=pltpu.VMEM)] * 2,
+            out_specs=[pl.BlockSpec(memory_space=pltpu.HBM)] * 2,
+            scratch_shapes=[pltpu.SemaphoreType.DMA((2,))],
+            name="put_out",
+        )(fine, coarse)
 
     spec = P("gx", "gy", None)
     return jax.shard_map(on_device, mesh=mesh, in_specs=(spec, spec), out_specs=(spec, spec), check_vma=False)

time: 51.8 us -> 49.6 us (0.958)
  local copies, waits for them, and re-layouts: 2.9 us -> 1.21 us
    pallas_call x1, Pallas kernels: 48 us -> 46.1 us  [on_device(): pl.pallas_call(lambda *refs: kernel(nx, ny, *refs), out_shape=(jax.ShapeD...]
    unnamed x6 -> x4, local copies, waits for them, and re-layouts: 2.9 us -> 1.21 us
    pallas_call x0 -> x1, Pallas kernels: none -> 1.49 us  [on_device(): pl.pallas_call(put_out, out_shape=(jax.ShapeDtypeStruct((8, 8, 256), F32)...]
where the time goes in v2:
time: 49.6 us; the launch traced here: 49.4 us
  Pallas kernels  47.6 us (96%)
  local copies, waits for them, and re-layouts  1.21 us (2%)
  between operations  0.65 us (1%)
    pallas_call x1, Pallas kernels, on_device(): pl.pallas_call(lambda *refs: kernel(nx, ny, *refs), out_shape=(jax.ShapeD...  46.1 us
    pallas_call x1, Pallas kernels, on_device(): pl.pallas_call(put_out, out_shape=(jax.ShapeDtypeStruct((8, 8, 256), F32)...  1.49 us
    unnamed x4, local copies, waits for them, and re-layouts  1.21 us

profile of v2, /device:TPU:1, one launch (start us, length us, event | category | flops | bytes accessed | tf_op | source)
XLA Modules:
  0.0 49.4 jit_solution(16477927398877373787)
XLA Ops:
  0.6 46.1 %vcycles.1 = (f32[8,8,256]{2,1,0:T(8,128)S(1)}, f32[4,4,128]{2,1,0:T(4,128)S(1)}) custom-call(f32[8,8,256]{2,1,0:T(8,128)} %refs_0_.1, f32[8,8,256]{2,1,0:T(8,128)} %refs_1_.1), custom_call_target="tpu_custom_call" | custom-call | tf_op jit(solution)/shard_map/vcycles/pallas_call | solution.py:474
  46.7 0.0 copy-start
  46.7 0.6 %copy-done = f32[8,8,256]{2,1,0:T(8,128)} copy-done((f32[8,8,256]{2,1,0:T(8,128)}, f32[8,8,256]{2,1,0:T(8,128)S(1)}, u32[]{:S(2)}) %copy-start) | copy-done | bytes 65560
  47.3 0.0 copy-start.1
  47.3 0.6 %copy-done.1 = f32[4,4,128]{2,1,0:T(4,128)} copy-done((f32[4,4,128]{2,1,0:T(4,128)}, f32[4,4,128]{2,1,0:T(4,128)S(1)}, u32[]{:S(2)}) %copy-start.1) | copy-done | bytes 8216
  47.9 1.5 %put_out.1 = (f32[8,8,256]{2,1,0:T(8,128)}, f32[4,4,128]{2,1,0:T(4,128)}) custom-call(f32[8,8,256]{2,1,0:T(8,128)} %copy-done, f32[4,4,128]{2,1,0:T(4,128)} %copy-done.1), custom_call_target="tpu_custom_call" | custom-call | tf_op jit(solution)/shard_map/put_out/pallas_call | solution.py:485
Async XLA Ops:
  46.7 0.6 %copy-start = (f32[8,8,256]{2,1,0:T(8,128)}, f32[8,8,256]{2,1,0:T(8,128)S(1)}, u32[]{:S(2)}) copy-start(f32[8,8,256]{2,1,0:T(8,128)S(1)} %get-tuple-element.4.fine) | copy-start | bytes 196612
  47.3 0.6 %copy-start.1 = (f32[4,4,128]{2,1,0:T(4,128)}, f32[4,4,128]{2,1,0:T(4,128)S(1)}, u32[]{:S(2)}) copy-start(f32[4,4,128]{2,1,0:T(4,128)S(1)} %get-tuple-element.5.coarse) | copy-start | bytes 24580

commit v3 on v2

--- a/solution.py
+++ b/solution.py
@@ -12,13 +12,13 @@
 F32 = jnp.float32
 ROWS = 16
 
-INNER = [(dx, dy) for dx in (-1, 1, 0) for dy in (0, -1, 1) if (dx, dy) != (0, 0)]
+INNER = [(-1, -1), (-1, 1), (1, -1), (1, 1), (-1, 0), (1, 0), (0, -1), (0, 1)]
 AROUND = INNER + [
     (dx, dy) for dx in (-2, 2, -1, 1, 0) for dy in (-2, -1, 0, 1, 2) if max(abs(dx), abs(dy)) == 2
 ]
 
-(G_K0, G_S0, G_E1, G_K2, G_ZK, G_GK, G_B1, G_B2, G_ZB, G_GB, G_V0, G_V1, G_U2) = range(13)
-GROUPS = 13
+(G_K0, G_S0, G_E1, G_K2, G_KC, G_GK, G_B1, G_BF, G_BC, G_GB, G_V0, G_V1, G_U2, G_KD) = range(14)
+GROUPS = 14
 
 
 def span(step, size, rim):
@@ -58,7 +58,7 @@
 
 
 def kernel(nx, ny, src_hbm, kap_hbm, fine_ref, coarse_ref, K0, S0, V0, VA0, VB0, C0, E1, B1, V1, VA1, VB1, C1, M1,
-           K2, B2, U2, VA2, VB2, C2, M2, ZK, ZB, GK, GB, C3, R3, W3, P3, Q3, X3, S5, T5, D, local_sem, send_sem, recv_sem, word):
+           K2, U2, VA2, VB2, C2, M2, KC, BF, BC, KM, VC, WC, PF, PC, CC, ZK, ZB, GK, GB, C3, R3, W3, P3, Q3, X3, S5, T5, D, local_sem, send_sem, recv_sem, word):
     gx = lax.axis_index("gx")
     gy = lax.axis_index("gy")
     mesh_ids = pl.DeviceIdType.MESH
@@ -90,15 +90,40 @@
             total += cx * cy * (ref.shape[-1] // 128) * (lead[1] if lead else 1)
         return total
 
-    def ship_column(group, ref):
+    pieces = {0: (0, 2, 0), -1: (0, 2, 2), 1: (0, 2, 6), -2: (0, 1, 4), 2: (1, 1, 5)}
+
+    def ship_sides(group, ref):
+        total = 0
+        for dy in (-2, 2, -1, 1):
+            here, count, there = pieces[dy]
+            pltpu.make_async_remote_copy(
+                src_ref=ref.at[:, pl.ds(here, count), :], dst_ref=ref.at[:, pl.ds(there, count), :],
+                send_sem=send_sem.at[group], recv_sem=recv_sem.at[group],
+                device_id=peer(0, dy), device_id_type=mesh_ids,
+            ).start()
+            total += nx * count
+        return total
+
+    def ship_columns(group, ref, spread):
+        def pass_on(x, steps):
+            for dy in steps:
+                here, count, there = pieces[dy]
+                pltpu.make_async_remote_copy(
+                    src_ref=ref.at[pl.ds(gx, 1), pl.ds(here, count), :], dst_ref=ref.at[pl.ds(gx, 1), pl.ds(there, count), :],
+                    send_sem=send_sem.at[group], recv_sem=recv_sem.at[group],
+                    device_id=(x, peer(0, dy)[1]), device_id_type=mesh_ids,
+                ).start()
+
+        sides = [dy for dy in (-2, 2, -1, 1) if abs(dy) <= spread]
+
         def step(i, carry):
-            pltpu.make_async_remote_copy(
-                src_ref=ref.at[pl.ds(gx, 1)], dst_ref=ref.at[pl.ds(gx, 1)], send_sem=send_sem.at[group],
-                recv_sem=recv_sem.at[group], device_id=(lax.rem(gx + i, nx), gy), device_id_type=mesh_ids,
-            ).start()
+            far = nx // 2 + (1 - 2 * lax.rem(i, 2)) * ((i + 1) // 2)
+            pass_on(lax.rem(gx + far, nx), sides + [0])
             return carry
-        lax.fori_loop(1, nx, step, 0)
-        return nx - 1
+
+        lax.fori_loop(0, nx - 1, step, 0)
+        pass_on(gx, sides)
+        return 2 * (nx - 1) + nx * sum(pieces[dy][1] for dy in sides)
 
     def ship_row(group, ref):
         def step(i, carry):
@@ -140,7 +165,7 @@
     n_s0 = ship(G_S0, S0, None, INNER, 8, 2, 1, 2)
     if nx > 2 * REACH:
         for dx in (REACH, -REACH):
-            pl.semaphore_signal(word, inc=1, device_id=peer(dx, 0), device_id_type=mesh_ids)
+            pl.semaphore_signal(word.at[0], inc=1, device_id=peer(dx, 0), device_id_type=mesh_ids)
 
     def restrict0(ref, offset, scale):
         out = []
@@ -159,8 +184,7 @@
     for i in range(2):
         own2.append(0.125 * pair_rows(pair_lanes(own1[2 * i] + own1[2 * i + 1], None)))
         K2[4 + i, 0:2, :] = own2[i][0:2]
-    both = own2[0] + own2[1]
-    ZK[pl.ds(gx, 1), :] = 0.125 * pair_rows(pair_lanes(both, None))[0:1]
+    KC[pl.ds(gx, 1), 0:2, :] = jnp.where(iota((8, 128), 1) < 64, own2[0], own2[1])[None, 0:2]
 
     def inside(shape, first, size, rim):
         plane = iota(shape, 0) + first + gx * size
@@ -211,6 +235,10 @@
 
     wait_group(G_K0, n_k0)
     n_k2 = ship(G_K2, K2, None, AROUND, 2, 4, 4, 4)
+    if nx > 2 * REACH:
+        pl.semaphore_wait(word.at[0], 2)
+    for dy in (-1, 1):
+        pl.semaphore_signal(word.at[1], inc=1, device_id=peer(0, dy), device_id_type=mesh_ids)
 
     def read_k0(a, n):
         k = K0[a:a + n]
@@ -242,9 +270,7 @@
         both = r[0] + r[1]
         B1[3 + i, 0:4, :] = 0.5 * pair_rows(pair_lanes(both[:, :128], both[:, 128:]))[0:4]
     n_b1 = ship(G_B1, B1, None, INNER, 4, 2, 2, 3)
-    if nx > 2 * REACH:
-        pl.semaphore_wait(word, 2)
-    n_zk = ship_column(G_ZK, ZK)
+    n_kc = ship_columns(G_KC, KC, 0)
     V0[2:10, 0:8, :] = VB0[1:9, 0:8, :]
 
 
@@ -269,18 +295,40 @@
         V1[k, 3:7, 0:4, :] = VB1[k, 1:5, 0:4, :]
         return r[0] + r[1], r[2] + r[3]
 
-    pairs_c = down1(1)
+    lane = iota((8, 128), 1)
+    sub = iota((8, 128), 0)
+
+    def right2(pairs, ref):
+        tiles = [0.5 * pair_rows(pair_lanes(x, None)) for x in pairs]
+        ref[pl.ds(gx, 1), 0:2, :] = jnp.where(lane < 64, tiles[0], tiles[1])[None, 0:2]
+        return tiles
+
+    tiles_c = right2(down1(1), BC)
+    pl.semaphore_wait(word.at[1], 2)
+    n_bc = ship_columns(G_BC, BC, 1)
     wait_group(G_B1, n_b1)
-    pairs_f = down1(0)
+    tiles_f = right2(down1(0), BF)
+    n_bf = ship_columns(G_BF, BF, 1)
     for i in range(2):
-        tile = 0.5 * pair_rows(pair_lanes(pairs_f[i], pairs_c[i]))
-        B2[2 + i, 0:2, :] = tile[0:2]
-        U2[0, 4 + i, 0:2, :] = tile[0:2]
-    n_b2 = ship(G_B2, B2, None, INNER, 2, 2, 2, 2)
-    wait_group(G_ZK, n_zk)
-    GK[gy] = packed(ZK)
-    n_gk = ship_row(G_GK, GK)
-
+        U2[0, 4 + i, 0:2, :] = jnp.where(lane < 64, tiles_f[i], tiles_c[i])[0:2]
+
+    even = lane < 64
+    deep = lax.rem(lane, 64)
+    row = jnp.where(sub < 5, sub, sub - 8) + 2 * gy
+    good2 = (row >= 0) & (row < 2 * ny)
+    blank = jnp.zeros((8, 128), F32)
+    chunk2 = min(8, nx)
+    for ref in (KM, VC, WC):
+        ref[0] = blank
+        ref[nx + 1] = blank
+
+    def beside_x(v):
+        n = v.shape[0] - 2
+        v = roll(v, 64, 2)
+        return jnp.where(even, v[0:n], v[1:n + 1]), jnp.where(even, v[1:n + 1], v[2:n + 2])
+
+    wait_group(G_KC, n_kc)
+    n_kd = ship_sides(G_KD, KC)
     wait_group(G_K2, n_k2)
 
     def read_k2(a, n):
@@ -288,16 +336,68 @@
         return jnp.where(inside(k.shape, a - 4, 2, 4), k, 0.0)
 
     faces(read_k2, C2, 8, 128, 64, 2, 4, -3, 4)
-    wait_group(G_B2, n_b2)
-    VA2[0:6] = C2[6, 1:7] * B2[0:6]
-    sweep(at(VA2, 2), 2, at(B2, 2), C2, 3, to(VB2, 1), -1, 4, 4)
-    r = residual(VB2[0:4], B2[2:4, 0:8], C2, 3, 2, 8)
-    U2[1, 4:6, 0:2, :] = VB2[1:3, 0:2, :]
-    ZB[pl.ds(gx, 1), :] = 0.5 * pair_rows(pair_lanes(r[0] + r[1], None))[0:1]
-    n_zb = ship_column(G_ZB, ZB)
+    wait_group(G_KD, n_kd)
+    for i in range(nx):
+        KM[1 + i] = jnp.where(good2, KC[i], 0.0)
+    for a in range(0, nx, chunk2):
+        k = KM[a:a + chunk2 + 2]
+        mid = k[1:chunk2 + 1]
+        previous, following = beside_x(k)
+        west, east = 0.5 * (mid + previous), 0.5 * (mid + following)
+        north = 0.5 * (mid + roll(mid, -1, 1))
+        south = roll(north, 1, 1)
+        above = 0.5 * (mid + jnp.where(deep == 63, 0.0, roll(mid, -1, 2)))
+        below = 0.5 * (mid + jnp.where(deep == 0, 0.0, roll(mid, 1, 2)))
+        total = west + east + north + south + above + below
+        CC[0, a:a + chunk2] = west
+        CC[1, a:a + chunk2] = east
+        CC[2, a:a + chunk2] = north
+        CC[3, a:a + chunk2] = south
+        CC[4, a:a + chunk2] = jnp.where(deep == 63, 0.0, above)
+        CC[5, a:a + chunk2] = jnp.where(deep == 0, 0.0, below)
+        CC[6, a:a + chunk2] = total
+        CC[7, a:a + chunk2] = jnp.where(good2, OMEGA / total, 0.0)
+
+    def pooled(tile):
+        tile = tile + roll(tile, 64, 1)
+        return tile + roll(tile, -1, 0)
+
+    for i in range(nx):
+        ZK[i:i + 1, :] = 0.125 * pair_lanes(pooled(KM[1 + i]), None)[0:1]
+
+    def packed(ref):
+        keep = sub + 8 * (lane // 64) < nx
+        return jnp.where(keep, jnp.where(lane < 64, ref[0:8], ref[8:16]), 0.0)
+
+    GK[gy] = packed(ZK)
+    n_gk = ship_row(G_GK, GK)
+
+    def residual2(V, b, a, n):
+        v = V[a:a + n + 2]
+        mid = v[1:n + 1]
+        previous, following = beside_x(v)
+        c = [CC[j, a:a + n] for j in range(7)]
+        beside = c[0] * previous + c[1] * following + c[2] * roll(mid, -1, 1) + c[3] * roll(mid, 1, 1)
+        beside += c[4] * roll(mid, -1, 2) + c[5] * roll(mid, 1, 2)
+        return b[a:a + n] - c[6] * mid + beside
+
+    def down2(b, summed):
+        for a in range(0, nx, chunk2):
+            VC[1 + a:1 + a + chunk2] = CC[7, a:a + chunk2] * b[a:a + chunk2]
+        for a in range(0, nx, chunk2):
+            v = VC[1 + a:1 + a + chunk2] + CC[7, a:a + chunk2] * residual2(VC, b, a, chunk2)
+            WC[1 + a:1 + a + chunk2] = v
+        own = WC[pl.ds(1 + gx, 1)][0]
+        for a in range(0, nx, chunk2):
+            r = residual2(WC, b, a, chunk2)
+            for i in range(chunk2):
+                summed[a + i] = pooled(r[i])
+        return own
+
+    wait_group(G_BC, n_bc)
+    own_c = down2(BC, PC)
 
     shape = (8, 128)
-    sub, lane = iota(shape, 0), iota(shape, 1)
     half = lane // 64
     at_x = sub + 8 * half
     z = lax.rem(lane, 32)
@@ -311,9 +411,19 @@
         a = roll(v, 1, 1)
         return jnp.where(sub == 0, roll(a, 64, 2), a)
 
+    wait_group(G_BF, n_bf)
+    own_f = down2(BF, PF)
+    for i in range(nx):
+        ZB[i:i + 1, :] = 0.5 * pair_lanes(jnp.where(even, PF[i], PC[i]), None)[0:1]
+    GB[gy] = packed(ZB)
+    n_gb = ship_row(G_GB, GB)
+    U2[1, 4, 0:2, :] = jnp.where(even, own_f, roll(own_c, 64, 1))[0:2]
+    U2[1, 5, 0:2, :] = jnp.where(even, roll(own_f, 64, 1), own_c)[0:2]
+    n_v0 = ship(G_V0, V0, None, INNER, 8, 2, 1, 2)
+    n_v1 = ship(G_V1, V1, (0, 2), INNER, 4, 3, 3, 3)
+    n_u2 = ship(G_U2, U2, (0, 2), AROUND, 2, 4, 4, 4)
     wait_group(G_GK, n_gk)
     chunk3 = min(8, ny)
-    blank = jnp.zeros(shape, F32)
     for a in range(0, ny, chunk3):
         k = GK[a:a + chunk3]
         up_y = [GK[j] if j < ny else blank for j in range(a + 1, a + chunk3 + 1)]
@@ -333,13 +443,6 @@
         C3[6, a:a + chunk3] = y_next + y_previous + x_next + x_previous + z_next + z_previous
     R3[0] = blank
     R3[ny + 1] = blank
-
-    wait_group(G_ZB, n_zb)
-    GB[gy] = packed(ZB)
-    n_gb = ship_row(G_GB, GB)
-    n_v0 = ship(G_V0, V0, None, INNER, 8, 2, 1, 2)
-    n_v1 = ship(G_V1, V1, (0, 2), INNER, 4, 3, 3, 3)
-    n_u2 = ship(G_U2, U2, (0, 2), AROUND, 2, 4, 4, 4)
     for a in range(0, ny, chunk3):
         P3[a:a + chunk3] = jnp.zeros((chunk3,) + shape, F32)
         Q3[a:a + chunk3] = jnp.zeros((chunk3,) + shape, F32)
@@ -435,8 +538,8 @@
     sweep(at(VA0, 2), 2, at(S0, 2), C0, 2, to(VB0, 1), -1, 10, 2)
     sweep(at(VB0, 1), 1, at(S0, 2), C0, 2, to(fine_ref, 0), 0, 8, 2, 8)
 
-    for group, rows in ((G_K0, n_k0), (G_S0, n_s0), (G_E1, n_e1), (G_K2, n_k2), (G_ZK, n_zk), (G_GK, n_gk), (G_B1, n_b1),
-                        (G_B2, n_b2), (G_ZB, n_zb), (G_GB, n_gb), (G_V0, n_v0), (G_V1, n_v1), (G_U2, n_u2)):
+    for group, rows in ((G_K0, n_k0), (G_S0, n_s0), (G_E1, n_e1), (G_K2, n_k2), (G_KC, n_kc), (G_KD, n_kd), (G_GK, n_gk), (G_B1, n_b1),
+                        (G_BF, n_bf), (G_BC, n_bc), (G_GB, n_gb), (G_V0, n_v0), (G_V1, n_v1), (G_U2, n_u2)):
         wait_rows(rows, send_sem.at[group])
 
 
@@ -463,13 +566,16 @@
             vmem(7, 13, 16, 256),
             vmem(2, 10, 16, 128), vmem(10, 16, 128), vmem(2, 10, 16, 128), vmem(2, 8, 16, 128), vmem(2, 6, 16, 128),
             vmem(7, 9, 16, 128), vmem(2, 10, 16, 128),
-            vmem(10, 16, 128), vmem(6, 16, 128), vmem(2, 10, 16, 128), vmem(8, 16, 128), vmem(6, 16, 128),
+            vmem(10, 16, 128), vmem(2, 10, 16, 128), vmem(8, 16, 128), vmem(6, 16, 128),
             vmem(7, 9, 16, 128), vmem(10, 16, 128),
+            vmem(nx, 8, 128), vmem(nx, 8, 128), vmem(nx, 8, 128),
+            vmem(nx + 2, 8, 128), vmem(nx + 2, 8, 128), vmem(nx + 2, 8, 128),
+            vmem(nx, 8, 128), vmem(nx, 8, 128), vmem(8, nx, 8, 128),
             vmem(16, 128), vmem(16, 128), vmem(ny, 8, 128), vmem(ny, 8, 128),
             vmem(7, ny, 8, 128), vmem(ny + 2, 8, 128), vmem(ny, 8, 128), vmem(ny, 8, 128), vmem(ny, 8, 128),
             vmem(ny + 4, 8, 128), vmem(5, 24, 128), vmem(5, 16, 128),
             vmem(512, 128),
-            pltpu.SemaphoreType.DMA((2,)), pltpu.SemaphoreType.DMA((GROUPS,)), pltpu.SemaphoreType.DMA((GROUPS,)), pltpu.SemaphoreType.REGULAR,
+            pltpu.SemaphoreType.DMA((2,)), pltpu.SemaphoreType.DMA((GROUPS,)), pltpu.SemaphoreType.DMA((GROUPS,)), pltpu.SemaphoreType.REGULAR((2,)),
         ]
         fine, coarse = pl.pallas_call(
             lambda *refs: kernel(nx, ny, *refs),
@@ -488,6 +594,7 @@
             in_specs=[pl.BlockSpec(memory_space=pltpu.VMEM)] * 2,
             out_specs=[pl.BlockSpec(memory_space=pltpu.HBM)] * 2,
             scratch_shapes=[pltpu.SemaphoreType.DMA((2,))],
+            compiler_params=pltpu.CompilerParams(vmem_limit_bytes=4 * 1024 * 1024),
             name="put_out",
         )(fine, coarse)
 

time: 49.6 us -> 45.7 us (0.921)
  Pallas kernels: 47.6 us -> 45 us
  local copies, waits for them, and re-layouts: 1.21 us -> 0 us
    pallas_call x1, Pallas kernels: 46.1 us -> 44.3 us  [on_device(): pl.pallas_call(lambda *refs: kernel(nx, ny, *refs), out_shape=(jax.ShapeD...]
    unnamed x4 -> x0, local copies, waits for them, and re-layouts: 1.21 us -> none
    pallas_call x1, Pallas kernels: 1.49 us -> 0.65 us  [on_device(): pl.pallas_call(put_out, out_shape=(jax.ShapeDtypeStruct((8, 8, 256), F32)...]
where the time goes in v3:
time: 45.7 us; the launch traced here: 45.6 us
  Pallas kernels  45 us (98%)
  between operations  0.64 us (1%)
    pallas_call x1, Pallas kernels, on_device(): pl.pallas_call(lambda *refs: kernel(nx, ny, *refs), out_shape=(jax.ShapeD...  44.3 us

profile of v3, /device:TPU:1, one launch (start us, length us, event | category | flops | bytes accessed | tf_op | source)
XLA Modules:
  0.0 45.6 jit_solution(9595623092343034642)
XLA Ops:
  0.6 44.3 %vcycles.1 = (f32[8,8,256]{2,1,0:T(8,128)S(1)}, f32[4,4,128]{2,1,0:T(4,128)S(1)}) custom-call(f32[8,8,256]{2,1,0:T(8,128)} %refs_0_.1, f32[8,8,256]{2,1,0:T(8,128)} %refs_1_.1), custom_call_target="tpu_custom_call" | custom-call | tf_op jit(solution)/shard_map/vcycles/pallas_call | solution.py:580
  45.0 0.7 %put_out.1 = (f32[8,8,256]{2,1,0:T(8,128)}, f32[4,4,128]{2,1,0:T(4,128)}) custom-call(f32[8,8,256]{2,1,0:T(8,128)S(1)} %get-tuple-element.4.fine, f32[4,4,128]{2,1,0:T(4,128)S(1)} %get-tuple-element.5.coarse), custom_call_target="tpu_custom_call" | custom-call | tf_op jit(solution)/shard_map/put_out/pallas_call | solution.py:591

commit v4 on v3

--- a/solution.py
+++ b/solution.py
@@ -17,8 +17,8 @@
     (dx, dy) for dx in (-2, 2, -1, 1, 0) for dy in (-2, -1, 0, 1, 2) if max(abs(dx), abs(dy)) == 2
 ]
 
-(G_K0, G_S0, G_E1, G_K2, G_KC, G_GK, G_B1, G_BF, G_BC, G_GB, G_V0, G_V1, G_U2, G_KD) = range(14)
-GROUPS = 14
+(G_K0, G_S0, G_E1, G_K2, G_KC, G_GK, G_B1, G_BF, G_BC, G_GB, G_V0, G_V1, G_U2, G_KD, G_BD) = range(15)
+GROUPS = 15
 
 
 def span(step, size, rim):
@@ -92,9 +92,9 @@
 
     pieces = {0: (0, 2, 0), -1: (0, 2, 2), 1: (0, 2, 6), -2: (0, 1, 4), 2: (1, 1, 5)}
 
-    def ship_sides(group, ref):
+    def ship_sides(group, ref, steps):
         total = 0
-        for dy in (-2, 2, -1, 1):
+        for dy in steps:
             here, count, there = pieces[dy]
             pltpu.make_async_remote_copy(
                 src_ref=ref.at[:, pl.ds(here, count), :], dst_ref=ref.at[:, pl.ds(there, count), :],
@@ -157,15 +157,8 @@
     for dx, dy in corners:
         greet(peer(dx, dy))
     lax.fori_loop(1, ny, greet_y, 0)
-    pl.semaphore_wait(barrier, len(near) + ny - 1 + len(corners))
     for copy in copies:
         copy.wait()
-
-    n_k0 = ship(G_K0, K0, None, INNER, 8, 3, 2, 3)
-    n_s0 = ship(G_S0, S0, None, INNER, 8, 2, 1, 2)
-    if nx > 2 * REACH:
-        for dx in (REACH, -REACH):
-            pl.semaphore_signal(word.at[0], inc=1, device_id=peer(dx, 0), device_id_type=mesh_ids)
 
     def restrict0(ref, offset, scale):
         out = []
@@ -179,12 +172,19 @@
         E1[1, 3 + i, 0:4, :] = tile[0:4]
     for i, tile in enumerate(restrict0(S0, 2, 0.5)):
         E1[0, 3 + i, 0:4, :] = tile[0:4]
-    n_e1 = ship(G_E1, E1, (0, 2), INNER, 4, 3, 3, 3)
     own2 = []
     for i in range(2):
         own2.append(0.125 * pair_rows(pair_lanes(own1[2 * i] + own1[2 * i + 1], None)))
         K2[4 + i, 0:2, :] = own2[i][0:2]
     KC[pl.ds(gx, 1), 0:2, :] = jnp.where(iota((8, 128), 1) < 64, own2[0], own2[1])[None, 0:2]
+
+    pl.semaphore_wait(barrier, len(near) + ny - 1 + len(corners))
+    n_k0 = ship(G_K0, K0, None, INNER, 8, 3, 2, 3)
+    n_s0 = ship(G_S0, S0, None, INNER, 8, 2, 1, 2)
+    if nx > 2 * REACH:
+        for dx in (REACH, -REACH):
+            pl.semaphore_signal(word.at[0], inc=1, device_id=peer(dx, 0), device_id_type=mesh_ids)
+    n_e1 = ship(G_E1, E1, (0, 2), INNER, 4, 3, 3, 3)
 
     def inside(shape, first, size, rim):
         plane = iota(shape, 0) + first + gx * size
@@ -304,10 +304,10 @@
         return tiles
 
     tiles_c = right2(down1(1), BC)
-    pl.semaphore_wait(word.at[1], 2)
-    n_bc = ship_columns(G_BC, BC, 1)
+    n_bc = ship_columns(G_BC, BC, 0)
     wait_group(G_B1, n_b1)
     tiles_f = right2(down1(0), BF)
+    pl.semaphore_wait(word.at[1], 2)
     n_bf = ship_columns(G_BF, BF, 1)
     for i in range(2):
         U2[0, 4 + i, 0:2, :] = jnp.where(lane < 64, tiles_f[i], tiles_c[i])[0:2]
@@ -328,7 +328,11 @@
         return jnp.where(even, v[0:n], v[1:n + 1]), jnp.where(even, v[1:n + 1], v[2:n + 2])
 
     wait_group(G_KC, n_kc)
-    n_kd = ship_sides(G_KD, KC)
+    n_kd = ship_sides(G_KD, KC, (-2, 2, -1, 1))
+    wait_group(G_BC, n_bc)
+    n_bd = ship_sides(G_BD, BC, (-1, 1))
+    n_v0 = ship(G_V0, V0, None, INNER, 8, 2, 1, 2)
+    n_v1 = ship(G_V1, V1, (0, 2), INNER, 4, 3, 3, 3)
     wait_group(G_K2, n_k2)
 
     def read_k2(a, n):
@@ -394,7 +398,7 @@
                 summed[a + i] = pooled(r[i])
         return own
 
-    wait_group(G_BC, n_bc)
+    wait_group(G_BD, n_bd)
     own_c = down2(BC, PC)
 
     shape = (8, 128)
@@ -419,8 +423,6 @@
     n_gb = ship_row(G_GB, GB)
     U2[1, 4, 0:2, :] = jnp.where(even, own_f, roll(own_c, 64, 1))[0:2]
     U2[1, 5, 0:2, :] = jnp.where(even, roll(own_f, 64, 1), own_c)[0:2]
-    n_v0 = ship(G_V0, V0, None, INNER, 8, 2, 1, 2)
-    n_v1 = ship(G_V1, V1, (0, 2), INNER, 4, 3, 3, 3)
     n_u2 = ship(G_U2, U2, (0, 2), AROUND, 2, 4, 4, 4)
     wait_group(G_GK, n_gk)
     chunk3 = min(8, ny)
@@ -538,7 +540,7 @@
     sweep(at(VA0, 2), 2, at(S0, 2), C0, 2, to(VB0, 1), -1, 10, 2)
     sweep(at(VB0, 1), 1, at(S0, 2), C0, 2, to(fine_ref, 0), 0, 8, 2, 8)
 
-    for group, rows in ((G_K0, n_k0), (G_S0, n_s0), (G_E1, n_e1), (G_K2, n_k2), (G_KC, n_kc), (G_KD, n_kd), (G_GK, n_gk), (G_B1, n_b1),
+    for group, rows in ((G_K0, n_k0), (G_S0, n_s0), (G_E1, n_e1), (G_K2, n_k2), (G_KC, n_kc), (G_KD, n_kd), (G_BD, n_bd), (G_GK, n_gk), (G_B1, n_b1),
                         (G_BF, n_bf), (G_BC, n_bc), (G_GB, n_gb), (G_V0, n_v0), (G_V1, n_v1), (G_U2, n_u2)):
         wait_rows(rows, send_sem.at[group])
 

time: 45.7 us -> 45.4 us (level)
  no operation moved by 1% of the time
where the time goes in v4:
time: 45.4 us; the launch traced here: 45.3 us
  Pallas kernels  44.6 us (98%)
  between operations  0.64 us (1%)
    pallas_call x1, Pallas kernels, on_device(): pl.pallas_call(lambda *refs: kernel(nx, ny, *refs), out_shape=(jax.ShapeD...  44 us

profile of v4, /device:TPU:1, one launch (start us, length us, event | category | flops | bytes accessed | tf_op | source)
XLA Modules:
  0.0 45.3 jit_solution(4594371006450723490)
XLA Ops:
  0.6 44.0 %vcycles.1 = (f32[8,8,256]{2,1,0:T(8,128)S(1)}, f32[4,4,128]{2,1,0:T(4,128)S(1)}) custom-call(f32[8,8,256]{2,1,0:T(8,128)} %refs_0_.1, f32[8,8,256]{2,1,0:T(8,128)} %refs_1_.1), custom_call_target="tpu_custom_call" | custom-call | tf_op jit(solution)/shard_map/vcycles/pallas_call | solution.py:582
  44.6 0.7 %put_out.1 = (f32[8,8,256]{2,1,0:T(8,128)}, f32[4,4,128]{2,1,0:T(4,128)}) custom-call(f32[8,8,256]{2,1,0:T(8,128)S(1)} %get-tuple-element.4.fine, f32[4,4,128]{2,1,0:T(4,128)S(1)} %get-tuple-element.5.coarse), custom_call_target="tpu_custom_call" | custom-call | tf_op jit(solution)/shard_map/put_out/pallas_call | solution.py:593

commit v5 on v4

--- a/solution.py
+++ b/solution.py
@@ -146,17 +146,26 @@
     def greet(device):
         pl.semaphore_signal(barrier, inc=1, device_id=device, device_id_type=mesh_ids)
 
-    def greet_y(i, carry):
-        greet((gx, lax.rem(gy + i, ny)))
-        return carry
-
     near = range(1, nx) if nx <= 2 * REACH else [*range(1, REACH + 1), *range(nx - REACH, nx)]
+    near_row = range(1, ny) if ny <= 4 else [1, 2, ny - 2, ny - 1]
     corners = [(dx, dy) for dx, dy in INNER if dx and dy]
+    strides = [2 ** k for k in range(1, 8) if 2 ** k < ny // 2]
+
+    def tell_row(k):
+        if k < len(strides):
+            for dy in (strides[k], -strides[k]):
+                pl.semaphore_signal(word.at[2 + k], inc=1, device_id=peer(0, dy), device_id_type=mesh_ids)
+
+    def hear_row(k):
+        if k < len(strides):
+            pl.semaphore_wait(word.at[2 + k], 2)
+
+    for dx, dy in corners:
+        greet(peer(dx, dy))
     for dx in near:
         greet(peer(dx, 0))
-    for dx, dy in corners:
-        greet(peer(dx, dy))
-    lax.fori_loop(1, ny, greet_y, 0)
+    for dy in near_row:
+        greet(peer(0, dy))
     for copy in copies:
         copy.wait()
 
@@ -178,7 +187,8 @@
         K2[4 + i, 0:2, :] = own2[i][0:2]
     KC[pl.ds(gx, 1), 0:2, :] = jnp.where(iota((8, 128), 1) < 64, own2[0], own2[1])[None, 0:2]
 
-    pl.semaphore_wait(barrier, len(near) + ny - 1 + len(corners))
+    pl.semaphore_wait(barrier, len(near) + len(near_row) + len(corners))
+    tell_row(0)
     n_k0 = ship(G_K0, K0, None, INNER, 8, 3, 2, 3)
     n_s0 = ship(G_S0, S0, None, INNER, 8, 2, 1, 2)
     if nx > 2 * REACH:
@@ -235,6 +245,8 @@
 
     wait_group(G_K0, n_k0)
     n_k2 = ship(G_K2, K2, None, AROUND, 2, 4, 4, 4)
+    hear_row(0)
+    tell_row(1)
     if nx > 2 * REACH:
         pl.semaphore_wait(word.at[0], 2)
     for dy in (-1, 1):
@@ -309,6 +321,8 @@
     tiles_f = right2(down1(0), BF)
     pl.semaphore_wait(word.at[1], 2)
     n_bf = ship_columns(G_BF, BF, 1)
+    hear_row(1)
+    tell_row(2)
     for i in range(2):
         U2[0, 4 + i, 0:2, :] = jnp.where(lane < 64, tiles_f[i], tiles_c[i])[0:2]
 
@@ -373,6 +387,9 @@
         keep = sub + 8 * (lane // 64) < nx
         return jnp.where(keep, jnp.where(lane < 64, ref[0:8], ref[8:16]), 0.0)
 
+    for k in range(2, len(strides)):
+        hear_row(k)
+        tell_row(k + 1)
     GK[gy] = packed(ZK)
     n_gk = ship_row(G_GK, GK)
 
@@ -577,7 +594,7 @@
             vmem(7, ny, 8, 128), vmem(ny + 2, 8, 128), vmem(ny, 8, 128), vmem(ny, 8, 128), vmem(ny, 8, 128),
             vmem(ny + 4, 8, 128), vmem(5, 24, 128), vmem(5, 16, 128),
             vmem(512, 128),
-            pltpu.SemaphoreType.DMA((2,)), pltpu.SemaphoreType.DMA((GROUPS,)), pltpu.SemaphoreType.DMA((GROUPS,)), pltpu.SemaphoreType.REGULAR((2,)),
+            pltpu.SemaphoreType.DMA((2,)), pltpu.SemaphoreType.DMA((GROUPS,)), pltpu.SemaphoreType.DMA((GROUPS,)), pltpu.SemaphoreType.REGULAR((10,)),
         ]
         fine, coarse = pl.pallas_call(
             lambda *refs: kernel(nx, ny, *refs),

time: 45.4 us -> 44.7 us (0.985)
  Pallas kernels: 44.6 us -> 43.9 us
    pallas_call x1, Pallas kernels: 44 us -> 43.3 us  [on_device(): pl.pallas_call(lambda *refs: kernel(nx, ny, *refs), out_shape=(jax.ShapeD...]
where the time goes in v5:
time: 44.7 us; the launch traced here: 44.6 us
  Pallas kernels  43.9 us (98%)
  between operations  0.64 us (1%)
    pallas_call x1, Pallas kernels, on_device(): pl.pallas_call(lambda *refs: kernel(nx, ny, *refs), out_shape=(jax.ShapeD...  43.3 us

profile of v5, /device:TPU:1, one launch (start us, length us, event | category | flops | bytes accessed | tf_op | source)
XLA Modules:
  0.0 44.6 jit_solution(17980338671772423706)
XLA Ops:
  0.6 43.3 %vcycles.1 = (f32[8,8,256]{2,1,0:T(8,128)S(1)}, f32[4,4,128]{2,1,0:T(4,128)S(1)}) custom-call(f32[8,8,256]{2,1,0:T(8,128)} %refs_0_.1, f32[8,8,256]{2,1,0:T(8,128)} %refs_1_.1), custom_call_target="tpu_custom_call" | custom-call | tf_op jit(solution)/shard_map/vcycles/pallas_call | solution.py:599
  43.9 0.7 %put_out.1 = (f32[8,8,256]{2,1,0:T(8,128)}, f32[4,4,128]{2,1,0:T(4,128)}) custom-call(f32[8,8,256]{2,1,0:T(8,128)S(1)} %get-tuple-element.4.fine, f32[4,4,128]{2,1,0:T(4,128)S(1)} %get-tuple-element.5.coarse), custom_call_target="tpu_custom_call" | custom-call | tf_op jit(solution)/shard_map/put_out/pallas_call | solution.py:610

commit v6 on v5

--- a/solution.py
+++ b/solution.py
@@ -77,8 +77,8 @@
         total = 0
         for dx, dy in steps:
             reach = corner if dx and dy else rim
-            px, cx, qx = span(dx, size, reach)
-            py, cy, qy = span(dy, size, reach)
+            px, cx, qx = span(dx, size, reach[0])
+            py, cy, qy = span(dy, size, reach[1])
             here = (pl.ds(px + offset, cx), pl.ds(py, cy), slice(None))
             there = (pl.ds(qx + offset, cx), pl.ds(qy % ROWS, cy), slice(None))
             if lead is not None:
@@ -136,8 +136,8 @@
         return 8 * (ny - 1)
 
     copies = [
-        pltpu.make_async_copy(kap_hbm, K0.at[pl.ds(3, 8), pl.ds(0, 8), :], local_sem.at[0]),
-        pltpu.make_async_copy(src_hbm, S0.at[pl.ds(2, 8), pl.ds(0, 8), :], local_sem.at[1]),
+        pltpu.make_async_copy(kap_hbm, K0.at[pl.ds(5, 8), pl.ds(0, 8), :], local_sem.at[0]),
+        pltpu.make_async_copy(src_hbm, S0.at[pl.ds(4, 8), pl.ds(0, 8), :], local_sem.at[1]),
     ]
     for copy in copies:
         copy.start()
@@ -176,10 +176,10 @@
             out.append(scale * pair_rows(pair_lanes(both[:, :128], both[:, 128:])))
         return out
 
-    own1 = restrict0(K0, 3, 0.125)
+    own1 = restrict0(K0, 5, 0.125)
     for i, tile in enumerate(own1):
         E1[1, 3 + i, 0:4, :] = tile[0:4]
-    for i, tile in enumerate(restrict0(S0, 2, 0.5)):
+    for i, tile in enumerate(restrict0(S0, 4, 0.5)):
         E1[0, 3 + i, 0:4, :] = tile[0:4]
     own2 = []
     for i in range(2):
@@ -189,12 +189,12 @@
 
     pl.semaphore_wait(barrier, len(near) + len(near_row) + len(corners))
     tell_row(0)
-    n_k0 = ship(G_K0, K0, None, INNER, 8, 3, 2, 3)
-    n_s0 = ship(G_S0, S0, None, INNER, 8, 2, 1, 2)
+    n_k0 = ship(G_K0, K0, None, INNER, 8, (5, 3), (4, 3), 5)
+    n_s0 = ship(G_S0, S0, None, INNER, 8, (4, 2), (3, 2), 4)
     if nx > 2 * REACH:
         for dx in (REACH, -REACH):
             pl.semaphore_signal(word.at[0], inc=1, device_id=peer(dx, 0), device_id_type=mesh_ids)
-    n_e1 = ship(G_E1, E1, (0, 2), INNER, 4, 3, 3, 3)
+    n_e1 = ship(G_E1, E1, (0, 2), INNER, 4, (3, 3), (3, 3), 3)
 
     def inside(shape, first, size, rim):
         plane = iota(shape, 0) + first + gx * size
@@ -244,7 +244,7 @@
             store(p, n, v[1:n + 1, 0:rows] + C[6, p + co:p + co + n, 0:rows] * r)
 
     wait_group(G_K0, n_k0)
-    n_k2 = ship(G_K2, K2, None, AROUND, 2, 4, 4, 4)
+    n_k2 = ship(G_K2, K2, None, AROUND, 2, (4, 4), (4, 4), 4)
     hear_row(0)
     tell_row(1)
     if nx > 2 * REACH:
@@ -254,11 +254,11 @@
 
     def read_k0(a, n):
         k = K0[a:a + n]
-        return jnp.where(inside(k.shape, a - 3, 8, 3), k, 0.0)
-
-    faces(read_k0, C0, 12, 256, 256, 8, 3, -2, 2)
+        return jnp.where(inside(k.shape, a - 5, 8, 3), k, 0.0)
+
+    faces(read_k0, C0, 16, 256, 256, 8, 3, -4, 2)
     wait_group(G_S0, n_s0)
-    for a in range(0, 12, 2):
+    for a in range(0, 16, 2):
         VA0[a:a + 2] = C0[6, a:a + 2] * S0[a:a + 2]
 
     def at(ref, offset, lead=None):
@@ -276,14 +276,25 @@
                 ref[(lead,) + where] = x
         return store
 
-    sweep(at(VA0, 2), 2, at(S0, 2), C0, 2, to(VB0, 1), -1, 10, 2)
-    for i in range(4):
+    sweep(at(VA0, 4), 4, at(S0, 4), C0, 4, to(VB0, 3), -3, 14, 2)
+    for i in range(6):
         r = residual(VB0[2 * i:2 * i + 4], S0[2 + 2 * i:4 + 2 * i, 0:8], C0, 2 + 2 * i, 2, 8)
         both = r[0] + r[1]
-        B1[3 + i, 0:4, :] = 0.5 * pair_rows(pair_lanes(both[:, :128], both[:, 128:]))[0:4]
-    n_b1 = ship(G_B1, B1, None, INNER, 4, 2, 2, 3)
+        cells = 0.5 * pair_rows(pair_lanes(both[:, :128], both[:, 128:]))[0:4]
+        B1[2 + i, 0:4, :] = cells
+        if 1 <= i <= 4:
+            V1[2, 2 + i, 0:4, :] = cells
+    n_b1 = 0
+    for dx, dy, planes, rows, land, row in (
+        (0, 1, (2, 6), (2, 2), 2, 14), (0, -1, (2, 6), (0, 2), 2, 4), (1, 0, (5, 1), (0, 4), 1, 0), (-1, 0, (4, 1), (0, 4), 8, 0)
+    ):
+        pltpu.make_async_remote_copy(
+            src_ref=B1.at[pl.ds(*planes), pl.ds(*rows), :], dst_ref=B1.at[pl.ds(land, planes[1]), pl.ds(row, rows[1]), :],
+            send_sem=send_sem.at[G_B1], recv_sem=recv_sem.at[G_B1], device_id=peer(dx, dy), device_id_type=mesh_ids,
+        ).start()
+        n_b1 += planes[1] * rows[1]
     n_kc = ship_columns(G_KC, KC, 0)
-    V0[2:10, 0:8, :] = VB0[1:9, 0:8, :]
+    V0[2:10, 0:8, :] = VB0[3:11, 0:8, :]
 
 
     def packed(ref):
@@ -345,8 +356,8 @@
     n_kd = ship_sides(G_KD, KC, (-2, 2, -1, 1))
     wait_group(G_BC, n_bc)
     n_bd = ship_sides(G_BD, BC, (-1, 1))
-    n_v0 = ship(G_V0, V0, None, INNER, 8, 2, 1, 2)
-    n_v1 = ship(G_V1, V1, (0, 2), INNER, 4, 3, 3, 3)
+    n_v0 = ship(G_V0, V0, None, INNER, 8, (2, 2), (1, 1), 2)
+    n_v1 = ship(G_V1, V1, (0, 3), INNER, 4, (3, 3), (3, 3), 3)
     wait_group(G_K2, n_k2)
 
     def read_k2(a, n):
@@ -440,7 +451,7 @@
     n_gb = ship_row(G_GB, GB)
     U2[1, 4, 0:2, :] = jnp.where(even, own_f, roll(own_c, 64, 1))[0:2]
     U2[1, 5, 0:2, :] = jnp.where(even, roll(own_f, 64, 1), own_c)[0:2]
-    n_u2 = ship(G_U2, U2, (0, 2), AROUND, 2, 4, 4, 4)
+    n_u2 = ship(G_U2, U2, (0, 2), AROUND, 2, (4, 4), (4, 4), 4)
     wait_group(G_GK, n_gk)
     chunk3 = min(8, ny)
     for a in range(0, ny, chunk3):
@@ -532,6 +543,7 @@
             high = take_rows(take_lanes(e[8:16], index), row_high)
             v = V1[k, p1 + 3] + jnp.concatenate([low, high], axis=0)
             M1[k, p1 + 3:p1 + 4] = jnp.where(good, v[None], 0.0)
+    b1 = (at(V1, 3, 2), at(E1, 3, 0))
     for k in range(2):
         sweep(at(M1, 3, k), 3, b1[k], C1, 2, to(VA1, 2, k), -2, 8, 4)
     sweep(at(VA1, 2, 0), 2, b1[0], C1, 2, to(VB1, 1, 0), -1, 6, 6)
@@ -553,9 +565,9 @@
             pieces.append(jnp.concatenate([low, high], axis=0))
         e = jnp.concatenate(pieces, axis=1)
         v = V0[2 * p1 + 2:2 * p1 + 4] + e[None]
-        VA0[2 * p1 + 2:2 * p1 + 4] = jnp.where(inside(v.shape, 2 * p1, 8, 2), v, 0.0)
-    sweep(at(VA0, 2), 2, at(S0, 2), C0, 2, to(VB0, 1), -1, 10, 2)
-    sweep(at(VB0, 1), 1, at(S0, 2), C0, 2, to(fine_ref, 0), 0, 8, 2, 8)
+        VA0[2 * p1 + 4:2 * p1 + 6] = jnp.where(inside(v.shape, 2 * p1, 8, 2), v, 0.0)
+    sweep(at(VA0, 4), 4, at(S0, 4), C0, 4, to(VB0, 3), -1, 10, 2)
+    sweep(at(VB0, 3), 3, at(S0, 4), C0, 4, to(fine_ref, 0), 0, 8, 2, 8)
 
     for group, rows in ((G_K0, n_k0), (G_S0, n_s0), (G_E1, n_e1), (G_K2, n_k2), (G_KC, n_kc), (G_KD, n_kd), (G_BD, n_bd), (G_GK, n_gk), (G_B1, n_b1),
                         (G_BF, n_bf), (G_BC, n_bc), (G_GB, n_gb), (G_V0, n_v0), (G_V1, n_v1), (G_U2, n_u2)):
@@ -581,9 +593,9 @@
 
     def on_device(source, kappa):
         scratch = [
-            vmem(14, 16, 256), vmem(12, 16, 256), vmem(12, 16, 256), vmem(12, 16, 256), vmem(10, 16, 256),
-            vmem(7, 13, 16, 256),
-            vmem(2, 10, 16, 128), vmem(10, 16, 128), vmem(2, 10, 16, 128), vmem(2, 8, 16, 128), vmem(2, 6, 16, 128),
+            vmem(18, 16, 256), vmem(16, 16, 256), vmem(12, 16, 256), vmem(16, 16, 256), vmem(14, 16, 256),
+            vmem(7, 17, 16, 256),
+            vmem(2, 10, 16, 128), vmem(10, 16, 128), vmem(3, 10, 16, 128), vmem(2, 8, 16, 128), vmem(2, 6, 16, 128),
             vmem(7, 9, 16, 128), vmem(2, 10, 16, 128),
             vmem(10, 16, 128), vmem(2, 10, 16, 128), vmem(8, 16, 128), vmem(6, 16, 128),
             vmem(7, 9, 16, 128), vmem(10, 16, 128),

time: 44.7 us -> 44.6 us (level)
  no operation moved by 1% of the time
where the time goes in v6:
time: 44.6 us; the launch traced here: 44.4 us
  Pallas kernels  43.8 us (98%)
  between operations  0.64 us (1%)
    pallas_call x1, Pallas kernels, on_device(): pl.pallas_call(lambda *refs: kernel(nx, ny, *refs), out_shape=(jax.ShapeD...  43.1 us

profile of v6, /device:TPU:1, one launch (start us, length us, event | category | flops | bytes accessed | tf_op | source)
XLA Modules:
  0.0 44.4 jit_solution(14895480887211834681)
XLA Ops:
  0.6 43.1 %vcycles.1 = (f32[8,8,256]{2,1,0:T(8,128)S(1)}, f32[4,4,128]{2,1,0:T(4,128)S(1)}) custom-call(f32[8,8,256]{2,1,0:T(8,128)} %refs_0_.1, f32[8,8,256]{2,1,0:T(8,128)} %refs_1_.1), custom_call_target="tpu_custom_call" | custom-call | tf_op jit(solution)/shard_map/vcycles/pallas_call | solution.py:611
  43.8 0.7 %put_out.1 = (f32[8,8,256]{2,1,0:T(8,128)}, f32[4,4,128]{2,1,0:T(4,128)}) custom-call(f32[8,8,256]{2,1,0:T(8,128)S(1)} %get-tuple-element.4.fine, f32[4,4,128]{2,1,0:T(4,128)S(1)} %get-tuple-element.5.coarse), custom_call_target="tpu_custom_call" | custom-call | tf_op jit(solution)/shard_map/put_out/pallas_call | solution.py:622
